TPU v7x, 32 devices: a whole 2x2x4 slice. The times are simulated.
32 devices in a mesh: dp: 4 (over y, core), label: 8 (over z, x).
Axes of the slice: x: 2, y: 2, z: 4, core: 2. Of those that a mesh axis runs over, the one named last changes fastest.
Arguments:
- feats: bfloat16 [2048, 1024], P('dp'), may hold values from -2 to 2
- weights: bfloat16 [128, 256, 1024], P(('dp', 'label')), may hold values from -5 to 5
- shortlist: int32 [16, 16], replicated, may hold values from 0 to 127, as said below
- slot_of: int32 [128], replicated, may hold values from 0 to 127, as said below
- positives: int32 [2048, 8], P('dp'), may hold values from 0 to 32767, as said below
Outputs:
- loss: float32 [2048], P('dp')
- grad_feats: bfloat16 [2048, 1024], P('dp', 'label')
Inputs may be any that keep to these rules, and one draw needn't show every extreme that they name: `slot_of`: A permutation of the cluster ids: the slot of each cluster. For each index d of dp, its blocks d * 4 to d * 4 + 3: the first 2 of them together shortlist one cluster stored on each device (the device of slot s being s // 4 in the order of the weights' placement), each once, and the last 2 shortlist the same clusters, each once; so every such cluster is shortlisted by exactly two blocks of d. `positives`: an instance's 8 labels are different, and each lies in a cluster that the instance's block shortlists.
All inputs are finite; a program needn't handle non-finite values.
Results may differ from a plain program's by a relative error of at most 0.0034.
Values may be sent and summed in bfloat16 or wider, within the bound.
No kernel may reach another device: no remote copies, remote signals or barrier semaphores. Data moves between devices by JAX's collectives and lax.ppermute only.
A program may use at most 64 MiB of HBM per device.

v0:
```python
import functools

import jax
import jax.numpy as jnp
from jax import lax
from jax.experimental import pallas as pl
from jax.experimental.pallas import tpu as pltpu
from jax.sharding import PartitionSpec as P

BLK = 128
NEG_FILL = -1e30
VMEM_BYTES = 32 * 1024 * 1024
VMEM_PICK = 56 * 1024 * 1024


def divide(value, by):
    if by & (by - 1) == 0:
        return lax.shift_right_logical(value, jnp.int32(by.bit_length() - 1))
    return lax.div(value, jnp.int32(by))


def remainder(value, by):
    if by & (by - 1) == 0:
        return value & jnp.int32(by - 1)
    return lax.rem(value, jnp.int32(by))


def each_entry(count, short_count, body, carry):
    if count <= 64:
        for e in range(count):
            carry = body(e // short_count, e % short_count, carry)
        return carry
    step = lambda e, c: body(divide(e, short_count), remainder(e, short_count), c)
    return lax.fori_loop(0, count, step, carry)


def find_slots(sizes, wanted, lists_ref, slot_ref):
    lab_count, stored, block_count, short_count = sizes
    dp_index, lab_index = lax.axis_index("dp"), lax.axis_index("label")
    mine = dp_index * lab_count + lab_index
    found = []
    for k in wanted:
        base = (dp_index ^ k) * block_count

        def look(row, column, slot_here, base=base):
            slot = slot_ref[lists_ref[base + row, column]]
            return jnp.where(divide(slot, stored) == mine, remainder(slot, stored), slot_here)

        count = block_count // 2 * short_count
        found.append(each_entry(count, short_count, look, jnp.int32(0)))
    return found


def far_kernel(sizes, wanted, lists_hbm, slot_hbm, weights_ref, *rest):
    outs = rest[: len(wanted)]
    held, lists_ref, slot_ref, sems = rest[len(wanted) :]
    tables = [
        pltpu.make_async_copy(lists_hbm, lists_ref, sems.at[0]),
        pltpu.make_async_copy(slot_hbm, slot_ref, sems.at[1]),
    ]
    stage = pltpu.make_async_copy(weights_ref, held, sems.at[2])
    for copy in tables:
        copy.start()
    stage.start()
    for copy in tables:
        copy.wait()
    found = find_slots(sizes, wanted, lists_ref, slot_ref)
    stage.wait()
    copies = []
    for i, slot in enumerate(found):
        copies.append(pltpu.make_async_copy(held.at[slot], outs[i], sems.at[3 + i]))
        copies[-1].start()
    for copy in copies:
        copy.wait()


def near_kernel(sizes, lists_ref, slot_ref, weights_ref, table_ref, *rest):
    lab_count, stored, block_count, short_count = sizes
    outs, sems = rest[:-1], rest[-1]
    copies = []
    for k, slot in enumerate(find_slots(sizes, range(1), lists_ref, slot_ref)):
        copies.append(pltpu.make_async_copy(weights_ref.at[slot], outs[k], sems.at[k]))
        copies[-1].start()
    dp_index, lab_index = lax.axis_index("dp"), lax.axis_index("label")
    half = block_count // 2
    for side in range(2):

        def note(row, column, carry, side=side):
            block = side * half + row
            cluster = lists_ref[dp_index * block_count + block, column]
            device = divide(slot_ref[cluster], stored)

            @pl.when(remainder(device, lab_count) == lab_index)
            def _():
                entry = divide(device, lab_count) ^ dp_index
                table_ref[entry, 0] = cluster
                table_ref[entry, 1 + side] = jnp.int32(block)

            return carry

        each_entry(half * short_count, short_count, note, jnp.int32(0))
    for copy in copies:
        copy.wait()


def target_of(pos_ref, block, first, cluster_size):
    labels = lax.broadcasted_iota(jnp.int32, (cluster_size, BLK), 0) + first
    pos = pos_ref[block]
    hit = pos[0:1, :] == labels
    for p in range(1, pos.shape[0]):
        hit = hit | (pos[p : p + 1, :] == labels)
    return hit


def logit_kernel(slots, copies, table_ref, feats_ref, pos_ref, *rest):
    count = len(slots)
    rows = rest[:count]
    stats_in = rest[count] if slots[0] else None
    logits_ref, out_ref, stats_ref = rest[-3:]
    cluster_size = rows[0].shape[0]
    if stats_in is None:
        stats_ref[0] = jnp.full(stats_ref.shape[1:], NEG_FILL, jnp.float32)
        stats_ref[1] = jnp.zeros(stats_ref.shape[1:], jnp.float32)
        stats_ref[2] = jnp.zeros(stats_ref.shape[1:], jnp.float32)
    else:
        stats_ref[...] = stats_in[0]
    for s, ref in zip(slots, rows):
        first = table_ref[s, 0] * cluster_size
        for side in range(2):
            block = table_ref[s, 1 + side]
            logits = lax.dot_general(
                ref[...],
                feats_ref[block],
                (((1,), (1,)), ((), ())),
                preferred_element_type=jnp.float32,
            )
            logits_ref[s - slots[0], :, side * BLK : (side + 1) * BLK] = logits
            hit = target_of(pos_ref, block, first, cluster_size)
            highest = jnp.max(logits, axis=0, keepdims=True)
            total = jnp.sum(jnp.exp(logits - highest), axis=0, keepdims=True)
            positive = jnp.sum(jnp.where(hit, logits, 0.0), axis=0, keepdims=True)
            row = pl.ds(block, 1)
            before = stats_ref[0, row, :]
            after = jnp.maximum(before, highest)
            stats_ref[0, row, :] = after
            stats_ref[1, row, :] = stats_ref[1, row, :] * jnp.exp(before - after) + total * jnp.exp(
                highest - after
            )
            stats_ref[2, row, :] = stats_ref[2, row, :] + positive
    for i in range(copies):
        out_ref[i] = stats_ref[...]


def row_sums(stats_ref, lab_count):
    highest = stats_ref[0, 0]
    for i in range(1, lab_count):
        highest = jnp.maximum(highest, stats_ref[i, 0])
    summed = jnp.zeros_like(highest)
    positive = jnp.zeros_like(highest)
    for i in range(lab_count):
        summed = summed + stats_ref[i, 1] * jnp.exp(stats_ref[i, 0] - highest)
        positive = positive + stats_ref[i, 2]
    return highest + jnp.log(summed), positive


def add_slot(side, s, table_ref, pos_ref, logits_ref, rows_ref, lse_ref, total_ref, first_block):
    cluster_size = rows_ref.shape[0]
    pos_count = pos_ref.shape[1]
    block = table_ref[s, 1 + side]
    hit = target_of(pos_ref, block, table_ref[s, 0] * cluster_size, cluster_size)
    dlogit = jnp.exp(
        logits_ref[:, side * BLK : (side + 1) * BLK] - lse_ref[pl.ds(block, 1), :]
    ) - jnp.where(hit, 1.0 / pos_count, 0.0)
    total_ref[block - first_block] += lax.dot_general(
        dlogit.T.astype(jnp.bfloat16),
        rows_ref[...],
        (((1,), (0,)), ((), ())),
        preferred_element_type=jnp.float32,
    )


def half_kernel(side, groups, lab_count, table_ref, pos_ref, stats_ref, *rest):
    dp_count = groups[-1][-1] + 1
    logits_refs = rest[: len(groups)]
    rows = rest[len(groups) : len(groups) + dp_count]
    loss_ref, keep_ref, send_ref, lse_ref, total_ref = rest[len(groups) + dp_count :]
    lse, positive = row_sums(stats_ref, lab_count)
    lse_ref[...] = lse
    loss_ref[...] = lse - positive / pos_ref.shape[1]
    total_ref[...] = jnp.zeros_like(total_ref)
    half = total_ref.shape[0]
    for slots, logits_ref in zip(groups, logits_refs):
        for s in slots:
            add_slot(
                side,
                s,
                table_ref,
                pos_ref,
                logits_ref.at[s - slots[0]],
                rows[s],
                lse_ref,
                total_ref,
                side * half,
            )
    part = keep_ref.shape[2]
    lab_index = lax.axis_index("label")
    for j in range(lab_count // 2):
        mine = pl.ds(pl.multiple_of((lab_index ^ (2 * j)) * part, part), part)
        other = pl.ds(pl.multiple_of((lab_index ^ (2 * j + 1)) * part, part), part)
        for b in range(half):
            here = pl.ds(b * BLK, BLK)
            keep_ref[j, here, :] = total_ref[b, :, mine]
            send_ref[j, here, :] = total_ref[b, :, other].astype(jnp.bfloat16)


def pair_kernel(keep_ref, got_ref, *outs):
    outs[0][...] = keep_ref[0] + got_ref[0].astype(jnp.float32)
    for j in range(1, len(outs)):
        outs[j][...] = (keep_ref[j] + got_ref[j].astype(jnp.float32)).astype(jnp.bfloat16)


def last_kernel(count, *refs):
    out_ref = refs[-1]
    for h in range(len(refs[:-1]) // count):
        total = refs[h * count][...]
        for ref in refs[h * count + 1 : (h + 1) * count]:
            total = total + ref[...].astype(jnp.float32)
        rows = total.shape[0]
        out_ref[h * rows : (h + 1) * rows, :] = total.astype(jnp.bfloat16)


def grad_kernel(groups, lab_count, table_ref, pos_ref, stats_ref, *rest):
    dp_count = groups[-1][-1] + 1
    logits_refs = rest[: len(groups)]
    rows = rest[len(groups) : len(groups) + dp_count]
    loss_ref, out_ref, lse_ref, total_ref = rest[len(groups) + dp_count :]
    lse, positive = row_sums(stats_ref, lab_count)
    lse_ref[...] = lse
    loss_ref[...] = lse - positive / pos_ref.shape[1]
    total_ref[...] = jnp.zeros_like(total_ref)
    for slots, logits_ref in zip(groups, logits_refs):
        for s in slots:

            @pl.when(table_ref[s, 0] >= 0)
            def _(s=s, logits_ref=logits_ref.at[s - slots[0]]):
                for side in range(2):
                    add_slot(
                        side, s, table_ref, pos_ref, logits_ref, rows[s], lse_ref, total_ref, 0
                    )

    part = out_ref.shape[2]
    for j in range(lab_count):
        for b in range(total_ref.shape[0]):
            out_ref[j, b * BLK : (b + 1) * BLK, :] = total_ref[
                b, :, j * part : (j + 1) * part
            ].astype(jnp.bfloat16)


def smem():
    return pl.BlockSpec(memory_space=pltpu.SMEM)


def vmem():
    return pl.BlockSpec(memory_space=pltpu.VMEM)


def anywhere():
    return pl.BlockSpec(memory_space=pl.ANY)


def shards(feats, weights, shortlist, slot_of, positives):
    dp_count = lax.axis_size("dp")
    lab_count = lax.axis_size("label")
    stored, cluster_size, width = weights.shape
    inst_count = feats.shape[0]
    pos_count = positives.shape[1]
    block_count = inst_count // BLK
    short_count = shortlist.shape[1]
    params = pltpu.CompilerParams(vmem_limit_bytes=VMEM_BYTES)
    row_type = jax.ShapeDtypeStruct((cluster_size, width), weights.dtype)
    stat_shape = (3, block_count, BLK)

    sizes = (lab_count, stored, block_count, short_count)
    far = range(1, dp_count)
    far_rows = pl.pallas_call(
        functools.partial(far_kernel, sizes, far),
        out_shape=[row_type] * len(far),
        in_specs=[anywhere()] * 3,
        out_specs=[anywhere()] * len(far),
        scratch_shapes=[
            pltpu.VMEM(weights.shape, weights.dtype),
            pltpu.SMEM(shortlist.shape, jnp.int32),
            pltpu.SMEM(slot_of.shape, jnp.int32),
            pltpu.SemaphoreType.DMA((3 + len(far),)),
        ],
        compiler_params=pltpu.CompilerParams(vmem_limit_bytes=VMEM_PICK),
        name="pick_far",
    )(shortlist, slot_of, weights)
    table, *rows = pl.pallas_call(
        functools.partial(near_kernel, sizes),
        out_shape=[jax.ShapeDtypeStruct((dp_count, 4), jnp.int32)] + [row_type],
        in_specs=[smem(), smem(), anywhere()],
        out_specs=[smem(), vmem()],
        scratch_shapes=[pltpu.SemaphoreType.DMA((1,))],
        compiler_params=params,
        name="pick_near",
    )(shortlist, slot_of, weights)
    rows += far_rows
    for k in range(1, dp_count):
        rows[k] = lax.ppermute(rows[k], "dp", [(i, i ^ k) for i in range(dp_count)])

    feat_blocks = feats.reshape(block_count, BLK, width)
    pos_blocks = positives.reshape(block_count, BLK, pos_count).transpose(0, 2, 1)
    cuts = (0, dp_count // 2, dp_count * 3 // 4, dp_count)
    groups = [tuple(range(a, b)) for a, b in zip(cuts[:-1], cuts[1:])]
    kept = []
    stats = []
    for slots in groups:
        count = len(slots)
        copies = lab_count if slots is groups[-1] else 1
        logits, stats_out = pl.pallas_call(
            functools.partial(logit_kernel, slots, copies),
            out_shape=[
                jax.ShapeDtypeStruct((count, cluster_size, 2 * BLK), jnp.float32),
                jax.ShapeDtypeStruct((copies,) + stat_shape, jnp.float32),
            ],
            in_specs=[smem()] + [vmem()] * (2 + count + len(stats)),
            out_specs=[vmem(), vmem()],
            scratch_shapes=[pltpu.VMEM(stat_shape, jnp.float32)],
            compiler_params=params,
            cost_estimate=pl.CostEstimate(
                flops=count * 4 * BLK * cluster_size * width,
                bytes_accessed=count * cluster_size * width * 2,
                transcendentals=0,
            ),
            name="logits",
        )(table, feat_blocks, pos_blocks, *[rows[s] for s in slots], *stats)
        kept.append(logits)
        stats = [stats_out]

    all_stats = lax.all_to_all(stats[0], "label", split_axis=0, concat_axis=0, tiled=True)
    part = width // lab_count
    in_specs = [smem()] + [vmem()] * (2 + len(groups) + dp_count)
    operands = (table, pos_blocks, all_stats, *kept, *rows)
    loss_type = jax.ShapeDtypeStruct((block_count, BLK), jnp.float32)
    lse_scratch = pltpu.VMEM((block_count, BLK), jnp.float32)
    if part % 128 or lab_count % 2:
        loss, parts = pl.pallas_call(
            functools.partial(grad_kernel, groups, lab_count),
            out_shape=[
                loss_type,
                jax.ShapeDtypeStruct((lab_count, inst_count, part), jnp.bfloat16),
            ],
            in_specs=in_specs,
            out_specs=[vmem(), vmem()],
            scratch_shapes=[lse_scratch, pltpu.VMEM((block_count, BLK, width), jnp.float32)],
            compiler_params=params,
            name="grads",
        )(*operands)
        gathered = lax.all_to_all(parts, "label", split_axis=0, concat_axis=0, tiled=True)
        grads = jnp.sum(gathered.astype(jnp.float32), axis=0).astype(jnp.bfloat16)
        return loss.reshape(inst_count), grads

    pairs = lab_count // 2
    half_rows = inst_count // 2
    finals = []
    for side in range(2):
        loss, keep, send = pl.pallas_call(
            functools.partial(half_kernel, side, groups, lab_count),
            out_shape=[
                loss_type,
                jax.ShapeDtypeStruct((pairs, half_rows, part), jnp.float32),
                jax.ShapeDtypeStruct((pairs, half_rows, part), jnp.bfloat16),
            ],
            in_specs=in_specs,
            out_specs=[vmem()] * 3,
            scratch_shapes=[lse_scratch, pltpu.VMEM((block_count // 2, BLK, width), jnp.float32)],
            compiler_params=params,
            cost_estimate=pl.CostEstimate(
                flops=dp_count * 2 * BLK * cluster_size * width,
                bytes_accessed=dp_count * cluster_size * width * 2,
                transcendentals=0,
            ),
            name="grads",
        )(*operands)
        if side:
            send, got = lax.optimization_barrier((send, got))
        got = lax.ppermute(send, "label", [(i, i ^ 1) for i in range(lab_count)])
        own, *outgoing = pl.pallas_call(
            pair_kernel,
            out_shape=[jax.ShapeDtypeStruct((half_rows, part), jnp.float32)]
            + [jax.ShapeDtypeStruct((half_rows, part), jnp.bfloat16)] * (pairs - 1),
            in_specs=[vmem()] * 2,
            out_specs=[vmem()] * pairs,
            compiler_params=params,
            name="pair_sums",
        )(keep, got)
        finals.append(own)
        for j in range(1, pairs):
            hop = [(i, i ^ (2 * j)) for i in range(lab_count)]
            finals.append(lax.ppermute(outgoing[j - 1], "label", hop))
    grads = pl.pallas_call(
        functools.partial(last_kernel, pairs),
        out_shape=jax.ShapeDtypeStruct((inst_count, part), jnp.bfloat16),
        in_specs=[vmem()] * (2 * pairs),
        out_specs=vmem(),
        compiler_params=params,
        name="last_sums",
    )(*finals)
    return loss.reshape(inst_count), grads


def solution(mesh):
    in_specs = (P("dp", None), P(("dp", "label"), None, None), P(), P(), P("dp", None))
    out_specs = (P("dp"), P("dp", "label"))
    return jax.shard_map(shards, mesh=mesh, in_specs=in_specs, out_specs=out_specs, check_vma=False)
```

profile of v0, /device:TPU:0, one launch (start us, length us, event | category | flops | bytes accessed | tf_op | source)
XLA Modules:
  0.0 67.2 jit_solution(4602461498915667916)
XLA Ops:
  0.6 0.0 copy-start.1
  0.6 0.0 copy-start.3
  0.7 0.0 copy-start.4
  0.7 0.0 copy-start.2
  0.7 0.0 copy-start
  0.7 3.0 %pick_far.1 = (bf16[256,1024]{1,0:T(8,128)(2,1)}, bf16[256,1024]{1,0:T(8,128)(2,1)}, bf16[256,1024]{1,0:T(8,128)(2,1)}) custom-call(s32[16,16]{1,0:T(8,128)} %lists_hbm.1, s32[128]{0:T(128)} %slot_hbm.1, bf16[4,256,1024]{2,1,0:T(8,128)(2,1)} %weights_ref.3), custom_call_target="tpu_custom_call" | custom-call | tf_op jit(solution)/shard_map/pick_far/pallas_call | solution.py:285
  3.6 0.5 collective-permute-start.2
  4.2 2.6 %collective-permute-start.1 = (bf16[256,1024]{1,0:T(8,128)(2,1)}, bf16[256,1024]{1,0:T(8,128)(2,1)S(1)}, u32[]{:S(2)}, u32[]{:S(2)}) collective-permute-start(bf16[256,1024]{1,0:T(8,128)(2,1)} %get-tuple-element.29), channel_id=1, source_target_pairs={{0,16},{8,24},{16,0},{24,8},{1,17},{9,25},{17,1},{25,9},{2,18},{10... | collective-permute-start | bytes 1572872 | tf_op jit(solution)/shard_map/ppermute | solution.py:310
  6.8 0.1 collective-permute-start
  6.8 0.0 copy-done.1
  6.8 0.0 copy-done.3
  6.8 0.0 copy-done.4
  6.8 1.6 %pick_near.1 = (s32[4,4]{1,0:T(4,128)S(1)}, bf16[256,1024]{1,0:T(8,128)(2,1)S(1)}) custom-call(s32[16,16]{1,0:T(8,128)S(1)} %copy-done.3, s32[128]{0:T(128)S(1)} %copy-done.4, bf16[4,256,1024]{2,1,0:T(8,128)(2,1)S(1)} %copy-done.1), custom_call_target="tpu_custom_call" | custom-call | tf_op jit(solution)/shard_map/pick_near/pallas_call | solution.py:299
  8.5 0.0 collective-permute-done.2.rest_1_.rest_4_
  8.5 0.0 copy-done.2
  8.5 0.0 copy-done
  8.5 1.6 %logits.3 = (f32[2,256,256]{2,1,0:T(8,128)S(1)}, f32[1,3,4,128]{3,2,1,0:T(4,128)S(1)}) custom-call(s32[4,4]{1,0:T(4,128)S(1)} %get-tuple-element.27.table_ref, bf16[4,128,1024]{2,1,0:T(8,128)(2,1)S(1)} %bitcast.5, s32[4,8,128]{2,1,0:T(8,128)S(1)} %bitcast.8, bf16[256,1024]{1,0:T(8,128)(2,1)S(1)} %get-tuple-element.30.rest_0_.rest_3_, ...), custom_call_target="tpu_custom_call" | custom-call | flops 268435456 | bytes 1048576 | tf_op jit(solution)/shard_map/logits/pallas_call | solution.py:321
  10.1 9.7 %collective-permute-done.1.rest_0_.rest_5_ = bf16[256,1024]{1,0:T(8,128)(2,1)S(1)} collective-permute-done((bf16[256,1024]{1,0:T(8,128)(2,1)}, bf16[256,1024]{1,0:T(8,128)(2,1)S(1)}, u32[]{:S(2)}, u32[]{:S(2)}) %collective-permute-start.1) | collective-permute-done | bytes 524320 | tf_op jit(solution)/shard_map/ppermute | solution.py:310
  19.7 1.1 %logits.4 = (f32[1,256,256]{2,1,0:T(8,128)S(1)}, f32[1,3,4,128]{3,2,1,0:T(4,128)S(1)}) custom-call(s32[4,4]{1,0:T(4,128)S(1)} %get-tuple-element.27.table_ref, bf16[4,128,1024]{2,1,0:T(8,128)(2,1)S(1)} %bitcast.6, s32[4,8,128]{2,1,0:T(8,128)S(1)} %bitcast.9, bf16[256,1024]{1,0:T(8,128)(2,1)S(1)} %collective-permute-done.1.rest_0_.rest_5_, ...), custom_call_target="tpu_custom_call" | custom-call | flops 134217728 | bytes 524288 | tf_op jit(solution)/shard_map/logits/pallas_call | solution.py:321
  20.9 9.6 %collective-permute-done.rest_0_.rest_6_ = bf16[256,1024]{1,0:T(8,128)(2,1)S(1)} collective-permute-done((bf16[256,1024]{1,0:T(8,128)(2,1)}, bf16[256,1024]{1,0:T(8,128)(2,1)S(1)}, u32[]{:S(2)}, u32[]{:S(2)}) %collective-permute-start) | collective-permute-done | bytes 524320 | tf_op jit(solution)/shard_map/ppermute | solution.py:310
  30.5 1.1 %logits.5 = (f32[1,256,256]{2,1,0:T(8,128)S(1)}, f32[8,3,4,128]{3,2,1,0:T(4,128)S(1)}) custom-call(s32[4,4]{1,0:T(4,128)S(1)} %get-tuple-element.27.table_ref, bf16[4,128,1024]{2,1,0:T(8,128)(2,1)S(1)} %bitcast.7, s32[4,8,128]{2,1,0:T(8,128)S(1)} %bitcast.10, bf16[256,1024]{1,0:T(8,128)(2,1)S(1)} %collective-permute-done.rest_0_.rest_6_, ...), custom_call_target="tpu_custom_call" | custom-call | flops 134217728 | bytes 524288 | tf_op jit(solution)/shard_map/logits/pallas_call | solution.py:321
  31.6 12.4 %all_to_all.5.stats_ref = f32[8,3,4,128]{3,2,1,0:T(4,128)S(1)} all-to-all(f32[8,3,4,128]{3,2,1,0:T(4,128)S(1)} %get-tuple-element.34), channel_id=1, replica_groups=mesh['dp'=4,'label'=8] {'label'}, dimensions={0} | all-to-all | bytes 98304 | tf_op jit(solution)/shard_map/all_to_all | solution.py:341
  44.0 2.0 %grads.3 = (f32[4,128]{1,0:T(4,128)}, f32[4,256,128]{2,1,0:T(8,128)S(1)}, bf16[4,256,128]{2,1,0:T(8,128)(2,1)S(1)}) custom-call(s32[4,4]{1,0:T(4,128)S(1)} %get-tuple-element.27.table_ref, s32[4,8,128]{2,1,0:T(8,128)S(1)} %bitcast.11, f32[8,3,4,128]{3,2,1,0:T(4,128)S(1)} %all_to_all.5.stats_ref, f32[2,256,256]{2,1,0:T(8,128)S(1)} %get-tuple-element.35.rest_0_, ...), custom_call_target="tpu_custom_call" | custom-call | flops 268435456 | bytes 2097152 | tf_op jit(solution)/shard_map/grads/pallas_call | solution.py:368
  46.1 0.4 collective-permute-start.3
  46.5 2.0 %grads.2 = (f32[4,128]{1,0:T(4,128)}, f32[4,256,128]{2,1,0:T(8,128)S(1)}, bf16[4,256,128]{2,1,0:T(8,128)(2,1)S(1)}) custom-call(s32[4,4]{1,0:T(4,128)S(1)} %get-tuple-element.27.table_ref, s32[4,8,128]{2,1,0:T(8,128)S(1)} %bitcast.12, f32[8,3,4,128]{3,2,1,0:T(4,128)S(1)} %all_to_all.5.stats_ref, f32[2,256,256]{2,1,0:T(8,128)S(1)} %get-tuple-element.35.rest_0_, ...), custom_call_target="tpu_custom_call" | custom-call | flops 268435456 | bytes 2097152 | tf_op jit(solution)/shard_map/grads/pallas_call | solution.py:368
  48.5 4.6 %collective-permute-done.3.got_ref = bf16[4,256,128]{2,1,0:T(8,128)(2,1)S(1)} collective-permute-done((bf16[4,256,128]{2,1,0:T(8,128)(2,1)S(1)}, bf16[4,256,128]{2,1,0:T(8,128)(2,1)S(1)}, u32[]{:S(2)}, u32[]{:S(2)}) %collective-permute-start.3) | collective-permute-done | bytes 262176 | tf_op jit(solution)/shard_map/ppermute | solution.py:388
  53.2 0.5 collective-permute-start.7
  53.7 0.8 %collective-permute-start.4 = (bf16[256,128]{1,0:T(8,128)(2,1)S(1)}, bf16[256,128]{1,0:T(8,128)(2,1)S(1)}, u32[]{:S(2)}, u32[]{:S(2)}) collective-permute-start(bf16[256,128]{1,0:T(8,128)(2,1)S(1)} %get-tuple-element.42), channel_id=1, source_target_pairs={{0,2},{1,3},{2,0},{3,1},{4,6},{5,7},{6,4},{7,5},{8,10},{9,11},{10,... | collective-permute-start | bytes 196616 | tf_op jit(solution)/shard_map/ppermute | solution.py:401
  54.5 0.8 %collective-permute-start.5 = (bf16[256,128]{1,0:T(8,128)(2,1)S(1)}, bf16[256,128]{1,0:T(8,128)(2,1)S(1)}, u32[]{:S(2)}, u32[]{:S(2)}) collective-permute-start(bf16[256,128]{1,0:T(8,128)(2,1)S(1)} %get-tuple-element.43), channel_id=1, source_target_pairs={{0,4},{1,5},{2,6},{3,7},{4,0},{5,1},{6,2},{7,3},{8,12},{9,13},{10,... | collective-permute-start | bytes 196616 | tf_op jit(solution)/shard_map/ppermute | solution.py:401
  55.4 2.8 %collective-permute-start.6 = (bf16[256,128]{1,0:T(8,128)(2,1)S(1)}, bf16[256,128]{1,0:T(8,128)(2,1)S(1)}, u32[]{:S(2)}, u32[]{:S(2)}) collective-permute-start(bf16[256,128]{1,0:T(8,128)(2,1)S(1)} %get-tuple-element.44), channel_id=1, source_target_pairs={{0,6},{1,7},{2,4},{3,5},{4,2},{5,3},{6,0},{7,1},{8,14},{9,15},{10,... | collective-permute-start | bytes 196616 | tf_op jit(solution)/shard_map/ppermute | solution.py:401
  58.2 1.4 %collective-permute-done.7.got_ref = bf16[4,256,128]{2,1,0:T(8,128)(2,1)S(1)} collective-permute-done((bf16[4,256,128]{2,1,0:T(8,128)(2,1)S(1)}, bf16[4,256,128]{2,1,0:T(8,128)(2,1)S(1)}, u32[]{:S(2)}, u32[]{:S(2)}) %collective-permute-start.7) | collective-permute-done | bytes 262176 | tf_op jit(solution)/shard_map/ppermute | solution.py:388
  59.5 0.1 pair_sums.3
  59.6 0.6 collective-permute-start.10
  60.2 0.6 collective-permute-start.8
  60.9 0.0 collective-permute-done.4.refs_1_
  60.9 3.2 %collective-permute-start.9 = (bf16[256,128]{1,0:T(8,128)(2,1)S(1)}, bf16[256,128]{1,0:T(8,128)(2,1)S(1)}, u32[]{:S(2)}, u32[]{:S(2)}) collective-permute-start(bf16[256,128]{1,0:T(8,128)(2,1)S(1)} %get-tuple-element.50), channel_id=1, source_target_pairs={{0,4},{1,5},{2,6},{3,7},{4,0},{5,1},{6,2},{7,3},{8,12},{9,13},{10,... | collective-permute-start | bytes 196616 | tf_op jit(solution)/shard_map/ppermute | solution.py:401
  64.1 0.0 collective-permute-done.5.refs_2_
  64.1 0.0 collective-permute-done.6.refs_3_
  64.1 1.7 %collective-permute-done.10.refs_7_ = bf16[256,128]{1,0:T(8,128)(2,1)S(1)} collective-permute-done((bf16[256,128]{1,0:T(8,128)(2,1)S(1)}, bf16[256,128]{1,0:T(8,128)(2,1)S(1)}, u32[]{:S(2)}, u32[]{:S(2)}) %collective-permute-start.10) | collective-permute-done | bytes 65568 | tf_op jit(solution)/shard_map/ppermute | solution.py:401
  65.8 0.0 collective-permute-done.8.refs_5_
  65.8 0.7 %collective-permute-done.9.refs_6_ = bf16[256,128]{1,0:T(8,128)(2,1)S(1)} collective-permute-done((bf16[256,128]{1,0:T(8,128)(2,1)S(1)}, bf16[256,128]{1,0:T(8,128)(2,1)S(1)}, u32[]{:S(2)}, u32[]{:S(2)}) %collective-permute-start.9) | collective-permute-done | bytes 65568 | tf_op jit(solution)/shard_map/ppermute | solution.py:401
  66.5 0.7 %last_sums.1 = bf16[512,128]{1,0:T(8,128)(2,1)} custom-call(f32[256,128]{1,0:T(8,128)S(1)} %get-tuple-element.41.refs_0_, bf16[256,128]{1,0:T(8,128)(2,1)S(1)} %collective-permute-done.4.refs_1_, bf16[256,128]{1,0:T(8,128)(2,1)S(1)} %collective-permute-done.5.refs_2_, bf16[256,128]{1,0:T(8,128)(2,1)S(1)} %collective-permute-done.6.refs_3_, ...), custom_call_target="tpu_custom_call" | custom-call | tf_op jit(solution)/shard_map/last_sums/pallas_call | solution.py:402
  (1 shorter events, 0.0 us)
Async XLA Ops:
  0.6 6.2 %copy-start.1 = (bf16[4,256,1024]{2,1,0:T(8,128)(2,1)S(1)}, bf16[4,256,1024]{2,1,0:T(8,128)(2,1)}, u32[]{:S(2)}) copy-start(bf16[4,256,1024]{2,1,0:T(8,128)(2,1)} %weights_ref.3) | copy-start | bytes 6291460
  0.6 6.2 %copy-start.3 = (s32[16,16]{1,0:T(8,128)S(1)}, s32[16,16]{1,0:T(8,128)}, u32[]{:S(2)}) copy-start(s32[16,16]{1,0:T(8,128)} %lists_hbm.1) | copy-start | bytes 3076
  0.7 6.2 %copy-start.4 = (s32[128]{0:T(128)S(1)}, s32[128]{0:T(128)}, u32[]{:S(2)}) copy-start(s32[128]{0:T(128)} %slot_hbm.1) | copy-start | bytes 1540
  0.7 7.8 %copy-start.2 = (s32[512,8]{0,1:T(8,128)S(1)}, s32[512,8]{0,1:T(8,128)}, u32[]{:S(2)}) copy-start(s32[512,8]{0,1:T(8,128)} %param.9) | copy-start | bytes 49156
  0.7 7.8 %copy-start = (bf16[512,1024]{1,0:T(8,128)(2,1)S(1)}, bf16[512,1024]{1,0:T(8,128)(2,1)}, u32[]{:S(2)}) copy-start(bf16[512,1024]{1,0:T(8,128)(2,1)} %param.5) | copy-start | bytes 3145732
  3.6 4.8 %collective-permute-start.2 = (bf16[256,1024]{1,0:T(8,128)(2,1)}, bf16[256,1024]{1,0:T(8,128)(2,1)S(1)}, u32[]{:S(2)}, u32[]{:S(2)}) collective-permute-start(bf16[256,1024]{1,0:T(8,128)(2,1)} %get-tuple-element.31), channel_id=1, source_target_pairs={{0,8},{8,0},{16,24},{24,16},{1,9},{9,1},{17,25},{25,17},{2,10},{10... | collective-permute-start | bytes 1572872 | tf_op jit(solution)/shard_map/ppermute | solution.py:310
  4.2 15.6 %collective-permute-start.1 = (bf16[256,1024]{1,0:T(8,128)(2,1)}, bf16[256,1024]{1,0:T(8,128)(2,1)S(1)}, u32[]{:S(2)}, u32[]{:S(2)}) collective-permute-start(bf16[256,1024]{1,0:T(8,128)(2,1)} %get-tuple-element.29), channel_id=1, source_target_pairs={{0,16},{8,24},{16,0},{24,8},{1,17},{9,25},{17,1},{25,9},{2,18},{10... | collective-permute-start | bytes 1572872 | tf_op jit(solution)/shard_map/ppermute | solution.py:310
  6.8 23.7 %collective-permute-start = (bf16[256,1024]{1,0:T(8,128)(2,1)}, bf16[256,1024]{1,0:T(8,128)(2,1)S(1)}, u32[]{:S(2)}, u32[]{:S(2)}) collective-permute-start(bf16[256,1024]{1,0:T(8,128)(2,1)} %get-tuple-element.28), channel_id=1, source_target_pairs={{0,24},{8,16},{16,8},{24,0},{1,25},{9,17},{17,9},{25,1},{2,26},{10... | collective-permute-start | bytes 1572872 | tf_op jit(solution)/shard_map/ppermute | solution.py:310
  46.1 7.1 %collective-permute-start.3 = (bf16[4,256,128]{2,1,0:T(8,128)(2,1)S(1)}, bf16[4,256,128]{2,1,0:T(8,128)(2,1)S(1)}, u32[]{:S(2)}, u32[]{:S(2)}) collective-permute-start(bf16[4,256,128]{2,1,0:T(8,128)(2,1)S(1)} %get-tuple-element.40), channel_id=1, source_target_pairs={{0,1},{1,0},{2,3},{3,2},{4,5},{5,4},{6,7},{7,6},{8,9},{9,8},{10,11... | collective-permute-start | bytes 786440 | tf_op jit(solution)/shard_map/ppermute | solution.py:388
  53.2 6.4 %collective-permute-start.7 = (bf16[4,256,128]{2,1,0:T(8,128)(2,1)S(1)}, bf16[4,256,128]{2,1,0:T(8,128)(2,1)S(1)}, u32[]{:S(2)}, u32[]{:S(2)}) collective-permute-start(bf16[4,256,128]{2,1,0:T(8,128)(2,1)S(1)} %get-tuple-element.47), channel_id=1, source_target_pairs={{0,1},{1,0},{2,3},{3,2},{4,5},{5,4},{6,7},{7,6},{8,9},{9,8},{10,11... | collective-permute-start | bytes 786440 | tf_op jit(solution)/shard_map/ppermute | solution.py:388
  53.7 7.2 %collective-permute-start.4 = (bf16[256,128]{1,0:T(8,128)(2,1)S(1)}, bf16[256,128]{1,0:T(8,128)(2,1)S(1)}, u32[]{:S(2)}, u32[]{:S(2)}) collective-permute-start(bf16[256,128]{1,0:T(8,128)(2,1)S(1)} %get-tuple-element.42), channel_id=1, source_target_pairs={{0,2},{1,3},{2,0},{3,1},{4,6},{5,7},{6,4},{7,5},{8,10},{9,11},{10,... | collective-permute-start | bytes 196616 | tf_op jit(solution)/shard_map/ppermute | solution.py:401
  54.5 9.5 %collective-permute-start.5 = (bf16[256,128]{1,0:T(8,128)(2,1)S(1)}, bf16[256,128]{1,0:T(8,128)(2,1)S(1)}, u32[]{:S(2)}, u32[]{:S(2)}) collective-permute-start(bf16[256,128]{1,0:T(8,128)(2,1)S(1)} %get-tuple-element.43), channel_id=1, source_target_pairs={{0,4},{1,5},{2,6},{3,7},{4,0},{5,1},{6,2},{7,3},{8,12},{9,13},{10,... | collective-permute-start | bytes 196616 | tf_op jit(solution)/shard_map/ppermute | solution.py:401
  55.4 8.7 %collective-permute-start.6 = (bf16[256,128]{1,0:T(8,128)(2,1)S(1)}, bf16[256,128]{1,0:T(8,128)(2,1)S(1)}, u32[]{:S(2)}, u32[]{:S(2)}) collective-permute-start(bf16[256,128]{1,0:T(8,128)(2,1)S(1)} %get-tuple-element.44), channel_id=1, source_target_pairs={{0,6},{1,7},{2,4},{3,5},{4,2},{5,3},{6,0},{7,1},{8,14},{9,15},{10,... | collective-permute-start | bytes 196616 | tf_op jit(solution)/shard_map/ppermute | solution.py:401
  59.6 6.2 %collective-permute-start.10 = (bf16[256,128]{1,0:T(8,128)(2,1)S(1)}, bf16[256,128]{1,0:T(8,128)(2,1)S(1)}, u32[]{:S(2)}, u32[]{:S(2)}) collective-permute-start(bf16[256,128]{1,0:T(8,128)(2,1)S(1)} %get-tuple-element.51), channel_id=1, source_target_pairs={{0,6},{1,7},{2,4},{3,5},{4,2},{5,3},{6,0},{7,1},{8,14},{9,15},{10,... | collective-permute-start | bytes 196616 | tf_op jit(solution)/shard_map/ppermute | solution.py:401
  60.2 5.6 %collective-permute-start.8 = (bf16[256,128]{1,0:T(8,128)(2,1)S(1)}, bf16[256,128]{1,0:T(8,128)(2,1)S(1)}, u32[]{:S(2)}, u32[]{:S(2)}) collective-permute-start(bf16[256,128]{1,0:T(8,128)(2,1)S(1)} %get-tuple-element.49), channel_id=1, source_target_pairs={{0,2},{1,3},{2,0},{3,1},{4,6},{5,7},{6,4},{7,5},{8,10},{9,11},{10,... | collective-permute-start | bytes 196616 | tf_op jit(solution)/shard_map/ppermute | solution.py:401
  60.9 5.6 %collective-permute-start.9 = (bf16[256,128]{1,0:T(8,128)(2,1)S(1)}, bf16[256,128]{1,0:T(8,128)(2,1)S(1)}, u32[]{:S(2)}, u32[]{:S(2)}) collective-permute-start(bf16[256,128]{1,0:T(8,128)(2,1)S(1)} %get-tuple-element.50), channel_id=1, source_target_pairs={{0,4},{1,5},{2,6},{3,7},{4,0},{5,1},{6,2},{7,3},{8,12},{9,13},{10,... | collective-permute-start | bytes 196616 | tf_op jit(solution)/shard_map/ppermute | solution.py:401
where the time goes:
time: 67.4 us; the launch traced here: 67.2 us
  waiting for transfers between devices  27.6 us (41%)
  Pallas kernels  13.3 us (20%)
  starting transfers between devices  13 us (19%)
  blocking collectives  12.4 us (18%)
  between operations  0.74 us (1%)
    ppermute x3, waiting for transfers between devices, shards(): rows[k] = lax.ppermute(rows[k], 'dp', [(i, i ^ k) for i in range(dp_count)])  19.2 us
    all_to_all x1, blocking collectives, shards(): lax.all_to_all(stats[0], 'label', split_axis=0, concat_axis=0, tiled=True)  12.4 us
    ppermute x6, starting transfers between devices, shards(): finals.append(lax.ppermute(outgoing[j - 1], 'label', hop))  8.91 us
    ppermute x2, waiting for transfers between devices, shards(): got = lax.ppermute(send, 'label', [(i, i ^ 1) for i in range(lab_count)])  6.01 us
    pallas_call x2, Pallas kernels, shards(): pl.pallas_call(functools.partial(half_kernel, side, groups, lab_count), o...  4.05 us
    pallas_call x3, Pallas kernels, shards(): pl.pallas_call(functools.partial(logit_kernel, slots, copies), out_shape=...  3.85 us
    ppermute x3, starting transfers between devices, shards(): rows[k] = lax.ppermute(rows[k], 'dp', [(i, i ^ k) for i in range(dp_count)])  3.18 us
    pallas_call x1, Pallas kernels, shards(): pl.pallas_call(functools.partial(far_kernel, sizes, far), out_shape=[row_...  2.95 us
  transfers between devices with their start and end apart: 11, of which 6 were waited for; matrix products, arithmetic and copies ran while one was open for 0% of the time, Pallas kernels for 10%

commit v1 on v0

--- a/solution.py
+++ b/solution.py
@@ -103,29 +103,38 @@
         copy.wait()
 
 
-def target_of(pos_ref, block, first, cluster_size):
-    labels = lax.broadcasted_iota(jnp.int32, (cluster_size, BLK), 0) + first
-    pos = pos_ref[block]
-    hit = pos[0:1, :] == labels
-    for p in range(1, pos.shape[0]):
-        hit = hit | (pos[p : p + 1, :] == labels)
-    return hit
-
-
-def logit_kernel(slots, copies, table_ref, feats_ref, pos_ref, *rest):
+def target_kernel(early, table_ref, pos_ref, hits_ref, shares_ref):
+    count, cluster_size, _ = hits_ref.shape
+    pos_count = pos_ref.shape[1]
+
+    def one_slot(s):
+        labels = lax.broadcasted_iota(jnp.int32, (cluster_size, BLK), 0) + table_ref[s, 0] * cluster_size
+        for side in range(2):
+            pos = pos_ref[table_ref[s, 1 + side]]
+            hit = pos[0:1, :] == labels
+            for p in range(1, pos_count):
+                hit = hit | (pos[p : p + 1, :] == labels)
+            hits = jnp.where(hit, 1.0, 0.0)
+            columns = pl.ds(side * BLK, BLK)
+            hits_ref[s, :, columns] = hits
+            if s in early:
+                shares_ref[early.index(s), columns, :] = (hits / pos_count).T
+
+    for s in range(count):
+        pl.when(table_ref[s, 0] >= 0)(functools.partial(one_slot, s))
+
+
+def logit_kernel(slots, turned, copies, table_ref, feats_ref, hits_ref, *rest):
     count = len(slots)
     rows = rest[:count]
-    stats_in = rest[count] if slots[0] else None
     logits_ref, out_ref, stats_ref = rest[-3:]
-    cluster_size = rows[0].shape[0]
-    if stats_in is None:
+    if len(rest) == count + 3:
         stats_ref[0] = jnp.full(stats_ref.shape[1:], NEG_FILL, jnp.float32)
         stats_ref[1] = jnp.zeros(stats_ref.shape[1:], jnp.float32)
         stats_ref[2] = jnp.zeros(stats_ref.shape[1:], jnp.float32)
     else:
-        stats_ref[...] = stats_in[0]
-    for s, ref in zip(slots, rows):
-        first = table_ref[s, 0] * cluster_size
+        stats_ref[...] = rest[count][0]
+    for i, (s, ref) in enumerate(zip(slots, rows)):
         for side in range(2):
             block = table_ref[s, 1 + side]
             logits = lax.dot_general(
@@ -134,11 +143,14 @@
                 (((1,), (1,)), ((), ())),
                 preferred_element_type=jnp.float32,
             )
-            logits_ref[s - slots[0], :, side * BLK : (side + 1) * BLK] = logits
-            hit = target_of(pos_ref, block, first, cluster_size)
+            columns = pl.ds(side * BLK, BLK)
+            if turned:
+                logits_ref[i, columns, :] = logits.T
+            else:
+                logits_ref[i, :, columns] = logits
             highest = jnp.max(logits, axis=0, keepdims=True)
             total = jnp.sum(jnp.exp(logits - highest), axis=0, keepdims=True)
-            positive = jnp.sum(jnp.where(hit, logits, 0.0), axis=0, keepdims=True)
+            positive = jnp.sum(hits_ref[s, :, columns] * logits, axis=0, keepdims=True)
             row = pl.ds(block, 1)
             before = stats_ref[0, row, :]
             after = jnp.maximum(before, highest)
@@ -163,45 +175,68 @@
     return highest + jnp.log(summed), positive
 
 
-def add_slot(side, s, table_ref, pos_ref, logits_ref, rows_ref, lse_ref, total_ref, first_block):
-    cluster_size = rows_ref.shape[0]
-    pos_count = pos_ref.shape[1]
-    block = table_ref[s, 1 + side]
-    hit = target_of(pos_ref, block, table_ref[s, 0] * cluster_size, cluster_size)
-    dlogit = jnp.exp(
-        logits_ref[:, side * BLK : (side + 1) * BLK] - lse_ref[pl.ds(block, 1), :]
-    ) - jnp.where(hit, 1.0 / pos_count, 0.0)
-    total_ref[block - first_block] += lax.dot_general(
-        dlogit.T.astype(jnp.bfloat16),
-        rows_ref[...],
-        (((1,), (0,)), ((), ())),
-        preferred_element_type=jnp.float32,
-    )
-
-
-def half_kernel(side, groups, lab_count, table_ref, pos_ref, stats_ref, *rest):
-    dp_count = groups[-1][-1] + 1
-    logits_refs = rest[: len(groups)]
-    rows = rest[len(groups) : len(groups) + dp_count]
-    loss_ref, keep_ref, send_ref, lse_ref, total_ref = rest[len(groups) + dp_count :]
+def prepare(stats_ref, pos_count, lab_count, loss_ref, lse_ref, columns_ref, total_ref, first):
     lse, positive = row_sums(stats_ref, lab_count)
     lse_ref[...] = lse
-    loss_ref[...] = lse - positive / pos_ref.shape[1]
+    loss_ref[...] = lse - positive / pos_count
+    for b in range(columns_ref.shape[0]):
+        columns_ref[b] = jnp.broadcast_to(lse[first + b : first + b + 1, :], (BLK, BLK)).T
     total_ref[...] = jnp.zeros_like(total_ref)
+
+
+def add_slots(sides, groups, pos_count, first, table_ref, hits_ref, shares_ref, logits_refs, rows, sums):
+    lse_ref, columns_ref, total_ref = sums
+    early = [s for slots in groups[:-1] for s in slots]
+    cluster_size = rows[0].shape[0]
+
+    def one_slot(s, logits_ref):
+        for side in sides:
+            block = table_ref[s, 1 + side]
+            here = pl.ds(side * BLK, BLK)
+            if s in early:
+                column = columns_ref[block - first]
+                column = jnp.concatenate([column] * (cluster_size // BLK), axis=1)
+                dlogit = jnp.exp(logits_ref[here, :] - column) - shares_ref[early.index(s), here, :]
+            else:
+                row = lse_ref[pl.ds(block, 1), :]
+                dlogit = jnp.exp(logits_ref[:, here] - row) - hits_ref[s, :, here] / pos_count
+                dlogit = dlogit.T
+            total_ref[block - first] += lax.dot_general(
+                dlogit.astype(jnp.bfloat16),
+                rows[s][...],
+                (((1,), (0,)), ((), ())),
+                preferred_element_type=jnp.float32,
+            )
+
+    for slots, logits_ref in zip(groups, logits_refs):
+        for i, s in enumerate(slots):
+            body = functools.partial(one_slot, s, logits_ref.at[i])
+            if len(rows) <= 4:
+                body()
+            else:
+                pl.when(table_ref[s, 0] >= 0)(body)
+
+
+def half_kernel(side, groups, lab_count, pos_count, table_ref, hits_ref, shares_ref, stats_ref, *rest):
+    logits_refs = rest[: len(groups)]
+    rows = rest[len(groups) : -6]
+    loss_ref, keep_ref, send_ref, lse_ref, columns_ref, total_ref = rest[-6:]
     half = total_ref.shape[0]
-    for slots, logits_ref in zip(groups, logits_refs):
-        for s in slots:
-            add_slot(
-                side,
-                s,
-                table_ref,
-                pos_ref,
-                logits_ref.at[s - slots[0]],
-                rows[s],
-                lse_ref,
-                total_ref,
-                side * half,
-            )
+    prepare(
+        stats_ref, pos_count, lab_count, loss_ref, lse_ref, columns_ref, total_ref, side * half
+    )
+    add_slots(
+        (side,),
+        groups,
+        pos_count,
+        side * half,
+        table_ref,
+        hits_ref,
+        shares_ref,
+        logits_refs,
+        rows,
+        (lse_ref, columns_ref, total_ref),
+    )
     part = keep_ref.shape[2]
     lab_index = lax.axis_index("label")
     for j in range(lab_count // 2):
@@ -229,25 +264,23 @@
         out_ref[h * rows : (h + 1) * rows, :] = total.astype(jnp.bfloat16)
 
 
-def grad_kernel(groups, lab_count, table_ref, pos_ref, stats_ref, *rest):
-    dp_count = groups[-1][-1] + 1
+def grad_kernel(groups, lab_count, pos_count, table_ref, hits_ref, shares_ref, stats_ref, *rest):
     logits_refs = rest[: len(groups)]
-    rows = rest[len(groups) : len(groups) + dp_count]
-    loss_ref, out_ref, lse_ref, total_ref = rest[len(groups) + dp_count :]
-    lse, positive = row_sums(stats_ref, lab_count)
-    lse_ref[...] = lse
-    loss_ref[...] = lse - positive / pos_ref.shape[1]
-    total_ref[...] = jnp.zeros_like(total_ref)
-    for slots, logits_ref in zip(groups, logits_refs):
-        for s in slots:
-
-            @pl.when(table_ref[s, 0] >= 0)
-            def _(s=s, logits_ref=logits_ref.at[s - slots[0]]):
-                for side in range(2):
-                    add_slot(
-                        side, s, table_ref, pos_ref, logits_ref, rows[s], lse_ref, total_ref, 0
-                    )
-
+    rows = rest[len(groups) : -5]
+    loss_ref, out_ref, lse_ref, columns_ref, total_ref = rest[-5:]
+    prepare(stats_ref, pos_count, lab_count, loss_ref, lse_ref, columns_ref, total_ref, 0)
+    add_slots(
+        (0, 1),
+        groups,
+        pos_count,
+        0,
+        table_ref,
+        hits_ref,
+        shares_ref,
+        logits_refs,
+        rows,
+        (lse_ref, columns_ref, total_ref),
+    )
     part = out_ref.shape[2]
     for j in range(lab_count):
         for b in range(total_ref.shape[0]):
@@ -313,15 +346,31 @@
     pos_blocks = positives.reshape(block_count, BLK, pos_count).transpose(0, 2, 1)
     cuts = (0, dp_count // 2, dp_count * 3 // 4, dp_count)
     groups = [tuple(range(a, b)) for a, b in zip(cuts[:-1], cuts[1:])]
+    if dp_count == 4:
+        groups = [(2,), (0, 1), (3,)]
+    early = [s for slots in groups[:-1] for s in slots]
+    hits, shares = pl.pallas_call(
+        functools.partial(target_kernel, early),
+        out_shape=[
+            jax.ShapeDtypeStruct((dp_count, cluster_size, 2 * BLK), jnp.float32),
+            jax.ShapeDtypeStruct((len(early), 2 * BLK, cluster_size), jnp.float32),
+        ],
+        in_specs=[smem(), vmem()],
+        out_specs=[vmem()] * 2,
+        compiler_params=params,
+        name="targets",
+    )(table, pos_blocks)
     kept = []
     stats = []
     for slots in groups:
         count = len(slots)
-        copies = lab_count if slots is groups[-1] else 1
+        last = slots is groups[-1]
+        copies = lab_count if last else 1
+        shape = (cluster_size, 2 * BLK) if last else (2 * BLK, cluster_size)
         logits, stats_out = pl.pallas_call(
-            functools.partial(logit_kernel, slots, copies),
+            functools.partial(logit_kernel, slots, not last, copies),
             out_shape=[
-                jax.ShapeDtypeStruct((count, cluster_size, 2 * BLK), jnp.float32),
+                jax.ShapeDtypeStruct((count,) + shape, jnp.float32),
                 jax.ShapeDtypeStruct((copies,) + stat_shape, jnp.float32),
             ],
             in_specs=[smem()] + [vmem()] * (2 + count + len(stats)),
@@ -334,26 +383,30 @@
                 transcendentals=0,
             ),
             name="logits",
-        )(table, feat_blocks, pos_blocks, *[rows[s] for s in slots], *stats)
+        )(table, feat_blocks, hits, *[rows[s] for s in slots], *stats)
         kept.append(logits)
         stats = [stats_out]
 
     all_stats = lax.all_to_all(stats[0], "label", split_axis=0, concat_axis=0, tiled=True)
     part = width // lab_count
-    in_specs = [smem()] + [vmem()] * (2 + len(groups) + dp_count)
-    operands = (table, pos_blocks, all_stats, *kept, *rows)
+    in_specs = [smem()] + [vmem()] * (3 + len(groups) + dp_count)
+    operands = (table, hits, shares, all_stats, *kept, *rows)
     loss_type = jax.ShapeDtypeStruct((block_count, BLK), jnp.float32)
     lse_scratch = pltpu.VMEM((block_count, BLK), jnp.float32)
     if part % 128 or lab_count % 2:
         loss, parts = pl.pallas_call(
-            functools.partial(grad_kernel, groups, lab_count),
+            functools.partial(grad_kernel, groups, lab_count, pos_count),
             out_shape=[
                 loss_type,
                 jax.ShapeDtypeStruct((lab_count, inst_count, part), jnp.bfloat16),
             ],
             in_specs=in_specs,
             out_specs=[vmem(), vmem()],
-            scratch_shapes=[lse_scratch, pltpu.VMEM((block_count, BLK, width), jnp.float32)],
+            scratch_shapes=[
+                lse_scratch,
+                pltpu.VMEM((block_count, BLK, BLK), jnp.float32),
+                pltpu.VMEM((block_count, BLK, width), jnp.float32),
+            ],
             compiler_params=params,
             name="grads",
         )(*operands)
@@ -366,7 +419,7 @@
     finals = []
     for side in range(2):
         loss, keep, send = pl.pallas_call(
-            functools.partial(half_kernel, side, groups, lab_count),
+            functools.partial(half_kernel, side, groups, lab_count, pos_count),
             out_shape=[
                 loss_type,
                 jax.ShapeDtypeStruct((pairs, half_rows, part), jnp.float32),
@@ -374,7 +427,11 @@
             ],
             in_specs=in_specs,
             out_specs=[vmem()] * 3,
-            scratch_shapes=[lse_scratch, pltpu.VMEM((block_count // 2, BLK, width), jnp.float32)],
+            scratch_shapes=[
+                lse_scratch,
+                pltpu.VMEM((block_count // 2, BLK, BLK), jnp.float32),
+                pltpu.VMEM((block_count // 2, BLK, width), jnp.float32),
+            ],
             compiler_params=params,
             cost_estimate=pl.CostEstimate(
                 flops=dp_count * 2 * BLK * cluster_size * width,

time: 67.4 us -> 66.8 us (level)
  waiting for transfers between devices: 27.6 us -> 26 us
  Pallas kernels: 13.3 us -> 14.4 us
    ppermute x3, waiting for transfers between devices: 19.2 us -> 16.6 us  [shards(): rows[k] = lax.ppermute(rows[k], 'dp', [(i, i ^ k) for i in range(dp_count)])]
    pallas_call x5 -> x6, Pallas kernels: 7.91 us -> 8.94 us  [the longest x2 3.62 us: shards(): pl.pallas_call(functools.partial(half_kernel, side, groups, lab_count, po...]
    ppermute x2, waiting for transfers between devices: 6.01 us -> 6.87 us  [shards(): got = lax.ppermute(send, 'label', [(i, i ^ 1) for i in range(lab_count)])]
  transfers between devices with their start and end apart: 11 -> 11, of which waited for: 6 -> 6; matrix products, arithmetic and copies ran while one was open for 0% -> 0% of each run, Pallas kernels for 10% -> 12%
where the time goes in v1:
time: 66.8 us; the launch traced here: 66.6 us
  waiting for transfers between devices  26 us (39%)
  Pallas kernels  14.4 us (22%)
  starting transfers between devices  13 us (19%)
  blocking collectives  12.4 us (19%)
  between operations  0.73 us (1%)
    ppermute x3, waiting for transfers between devices, shards(): rows[k] = lax.ppermute(rows[k], 'dp', [(i, i ^ k) for i in range(dp_count)])  16.6 us
    all_to_all x1, blocking collectives, shards(): lax.all_to_all(stats[0], 'label', split_axis=0, concat_axis=0, tiled=True)  12.4 us
    ppermute x6, starting transfers between devices, shards(): finals.append(lax.ppermute(outgoing[j - 1], 'label', hop))  8.91 us
    ppermute x2, waiting for transfers between devices, shards(): got = lax.ppermute(send, 'label', [(i, i ^ 1) for i in range(lab_count)])  6.87 us
    pallas_call x2, Pallas kernels, shards(): pl.pallas_call(functools.partial(half_kernel, side, groups, lab_count, po...  3.62 us
    pallas_call x3, Pallas kernels, shards(): pl.pallas_call(functools.partial(logit_kernel, slots, not last, copies),...  3.57 us
    ppermute x3, starting transfers between devices, shards(): rows[k] = lax.ppermute(rows[k], 'dp', [(i, i ^ k) for i in range(dp_count)])  3.24 us
    pallas_call x1, Pallas kernels, shards(): pl.pallas_call(functools.partial(far_kernel, sizes, far), out_shape=[row_...  2.97 us
  transfers between devices with their start and end apart: 11, of which 6 were waited for; matrix products, arithmetic and copies ran while one was open for 0% of the time, Pallas kernels for 12%

profile of v1, /device:TPU:0, one launch (start us, length us, event | category | flops | bytes accessed | tf_op | source)
XLA Modules:
  0.0 66.6 jit_solution(5187422060528364523)
XLA Ops:
  0.6 0.0 copy-start.1
  0.6 0.0 copy-start.2
  0.7 0.0 copy-start.4
  0.7 0.0 copy-start.3
  0.7 0.0 copy-start
  0.7 3.0 %pick_far.1 = (bf16[256,1024]{1,0:T(8,128)(2,1)}, bf16[256,1024]{1,0:T(8,128)(2,1)}, bf16[256,1024]{1,0:T(8,128)(2,1)}) custom-call(s32[16,16]{1,0:T(8,128)} %lists_hbm.1, s32[128]{0:T(128)} %slot_hbm.1, bf16[4,256,1024]{2,1,0:T(8,128)(2,1)} %weights_ref.3), custom_call_target="tpu_custom_call" | custom-call | tf_op jit(solution)/shard_map/pick_far/pallas_call | solution.py:318
  3.7 3.0 %collective-permute-start.2 = (bf16[256,1024]{1,0:T(8,128)(2,1)}, bf16[256,1024]{1,0:T(8,128)(2,1)S(1)}, u32[]{:S(2)}, u32[]{:S(2)}) collective-permute-start(bf16[256,1024]{1,0:T(8,128)(2,1)} %get-tuple-element.35), channel_id=1, source_target_pairs={{0,16},{8,24},{16,0},{24,8},{1,17},{9,25},{17,1},{25,9},{2,18},{10... | collective-permute-start | bytes 1572872 | tf_op jit(solution)/shard_map/ppermute | solution.py:343
  6.7 0.0 collective-permute-start.1
  6.7 0.2 collective-permute-start
  6.9 0.0 copy-done.1
  6.9 0.0 copy-done.2
  6.9 0.0 copy-done.4
  6.9 1.6 %pick_near.1 = (s32[4,4]{1,0:T(4,128)S(1)}, bf16[256,1024]{1,0:T(8,128)(2,1)S(1)}) custom-call(s32[16,16]{1,0:T(8,128)S(1)} %copy-done.2, s32[128]{0:T(128)S(1)} %copy-done.4, bf16[4,256,1024]{2,1,0:T(8,128)(2,1)S(1)} %copy-done.1), custom_call_target="tpu_custom_call" | custom-call | tf_op jit(solution)/shard_map/pick_near/pallas_call | solution.py:332
  8.6 0.0 copy-done.3
  8.6 1.7 %targets.1 = (f32[4,256,256]{2,1,0:T(8,128)S(1)}, f32[3,256,256]{2,1,0:T(8,128)S(1)}) custom-call(s32[4,4]{1,0:T(4,128)S(1)} %get-tuple-element.29.table_ref, s32[4,8,128]{2,1,0:T(8,128)S(1)} %bitcast.8), custom_call_target="tpu_custom_call" | custom-call | tf_op jit(solution)/shard_map/targets/pallas_call | solution.py:352
  10.3 9.3 %collective-permute-done.2.rest_0_.rest_5_ = bf16[256,1024]{1,0:T(8,128)(2,1)S(1)} collective-permute-done((bf16[256,1024]{1,0:T(8,128)(2,1)}, bf16[256,1024]{1,0:T(8,128)(2,1)S(1)}, u32[]{:S(2)}, u32[]{:S(2)}) %collective-permute-start.2) | collective-permute-done | bytes 524320 | tf_op jit(solution)/shard_map/ppermute | solution.py:343
  19.6 0.0 copy-done
  19.7 1.1 %logits.3 = (f32[1,256,256]{2,1,0:T(8,128)S(1)}, f32[1,3,4,128]{3,2,1,0:T(4,128)S(1)}) custom-call(s32[4,4]{1,0:T(4,128)S(1)} %get-tuple-element.29.table_ref, bf16[4,128,1024]{2,1,0:T(8,128)(2,1)S(1)} %bitcast.5, f32[4,256,256]{2,1,0:T(8,128)S(1)} %get-tuple-element.30.hits_ref, bf16[256,1024]{1,0:T(8,128)(2,1)S(1)} %collective-permute-done.2.rest_0_.rest_5_), custom_call_target="tpu_custom_call" | custom-call | flops 134217728 | bytes 524288 | tf_op jit(solution)/shard_map/logits/pallas_call | solution.py:370
  20.8 0.0 collective-permute-done.1.rest_1_.rest_4_
  20.8 1.4 %logits.4 = (f32[2,256,256]{2,1,0:T(8,128)S(1)}, f32[1,3,4,128]{3,2,1,0:T(4,128)S(1)}) custom-call(s32[4,4]{1,0:T(4,128)S(1)} %get-tuple-element.29.table_ref, bf16[4,128,1024]{2,1,0:T(8,128)(2,1)S(1)} %bitcast.6, f32[4,256,256]{2,1,0:T(8,128)S(1)} %get-tuple-element.30.hits_ref, bf16[256,1024]{1,0:T(8,128)(2,1)S(1)} %get-tuple-element.33.rest_0_.rest_3_, ...), custom_call_target="tpu_custom_call" | custom-call | flops 268435456 | bytes 1048576 | tf_op jit(solution)/shard_map/logits/pallas_call | solution.py:370
  22.2 7.3 %collective-permute-done.rest_0_.rest_6_ = bf16[256,1024]{1,0:T(8,128)(2,1)S(1)} collective-permute-done((bf16[256,1024]{1,0:T(8,128)(2,1)}, bf16[256,1024]{1,0:T(8,128)(2,1)S(1)}, u32[]{:S(2)}, u32[]{:S(2)}) %collective-permute-start) | collective-permute-done | bytes 524320 | tf_op jit(solution)/shard_map/ppermute | solution.py:343
  29.4 1.1 %logits.5 = (f32[1,256,256]{2,1,0:T(8,128)S(1)}, f32[8,3,4,128]{3,2,1,0:T(4,128)S(1)}) custom-call(s32[4,4]{1,0:T(4,128)S(1)} %get-tuple-element.29.table_ref, bf16[4,128,1024]{2,1,0:T(8,128)(2,1)S(1)} %bitcast.7, f32[4,256,256]{2,1,0:T(8,128)S(1)} %get-tuple-element.30.hits_ref, bf16[256,1024]{1,0:T(8,128)(2,1)S(1)} %collective-permute-done.rest_0_.rest_6_, ...), custom_call_target="tpu_custom_call" | custom-call | flops 134217728 | bytes 524288 | tf_op jit(solution)/shard_map/logits/pallas_call | solution.py:370
  30.5 12.4 %all_to_all.5.stats_ref = f32[8,3,4,128]{3,2,1,0:T(4,128)S(1)} all-to-all(f32[8,3,4,128]{3,2,1,0:T(4,128)S(1)} %get-tuple-element.38), channel_id=1, replica_groups=mesh['dp'=4,'label'=8] {'label'}, dimensions={0} | all-to-all | bytes 98304 | tf_op jit(solution)/shard_map/all_to_all | solution.py:390
  42.9 1.8 %grads.3 = (f32[4,128]{1,0:T(4,128)}, f32[4,256,128]{2,1,0:T(8,128)S(1)}, bf16[4,256,128]{2,1,0:T(8,128)(2,1)S(1)}) custom-call(s32[4,4]{1,0:T(4,128)S(1)} %get-tuple-element.29.table_ref, f32[4,256,256]{2,1,0:T(8,128)S(1)} %get-tuple-element.30.hits_ref, f32[3,256,256]{2,1,0:T(8,128)S(1)} %get-tuple-element.31.shares_ref, ...), custom_call_target="tpu_custom_call" | custom-call | flops 268435456 | bytes 2097152 | tf_op jit(solution)/shard_map/grads/pallas_call | solution.py:421
  44.7 0.4 collective-permute-start.3
  45.1 1.8 %grads.2 = (f32[4,128]{1,0:T(4,128)}, f32[4,256,128]{2,1,0:T(8,128)S(1)}, bf16[4,256,128]{2,1,0:T(8,128)(2,1)S(1)}) custom-call(s32[4,4]{1,0:T(4,128)S(1)} %get-tuple-element.29.table_ref, f32[4,256,256]{2,1,0:T(8,128)S(1)} %get-tuple-element.30.hits_ref, f32[3,256,256]{2,1,0:T(8,128)S(1)} %get-tuple-element.31.shares_ref, ...), custom_call_target="tpu_custom_call" | custom-call | flops 268435456 | bytes 2097152 | tf_op jit(solution)/shard_map/grads/pallas_call | solution.py:421
  47.0 5.2 %collective-permute-done.3.got_ref = bf16[4,256,128]{2,1,0:T(8,128)(2,1)S(1)} collective-permute-done((bf16[4,256,128]{2,1,0:T(8,128)(2,1)S(1)}, bf16[4,256,128]{2,1,0:T(8,128)(2,1)S(1)}, u32[]{:S(2)}, u32[]{:S(2)}) %collective-permute-start.3) | collective-permute-done | bytes 262176 | tf_op jit(solution)/shard_map/ppermute | solution.py:445
  52.2 0.4 collective-permute-start.7
  52.6 0.1 pair_sums.2
  52.7 0.8 %collective-permute-start.4 = (bf16[256,128]{1,0:T(8,128)(2,1)S(1)}, bf16[256,128]{1,0:T(8,128)(2,1)S(1)}, u32[]{:S(2)}, u32[]{:S(2)}) collective-permute-start(bf16[256,128]{1,0:T(8,128)(2,1)S(1)} %get-tuple-element.46), channel_id=1, source_target_pairs={{0,2},{1,3},{2,0},{3,1},{4,6},{5,7},{6,4},{7,5},{8,10},{9,11},{10,... | collective-permute-start | bytes 196616 | tf_op jit(solution)/shard_map/ppermute | solution.py:458
  53.5 1.0 %collective-permute-start.5 = (bf16[256,128]{1,0:T(8,128)(2,1)S(1)}, bf16[256,128]{1,0:T(8,128)(2,1)S(1)}, u32[]{:S(2)}, u32[]{:S(2)}) collective-permute-start(bf16[256,128]{1,0:T(8,128)(2,1)S(1)} %get-tuple-element.47), channel_id=1, source_target_pairs={{0,4},{1,5},{2,6},{3,7},{4,0},{5,1},{6,2},{7,3},{8,12},{9,13},{10,... | collective-permute-start | bytes 196616 | tf_op jit(solution)/shard_map/ppermute | solution.py:458
  54.5 2.6 %collective-permute-start.6 = (bf16[256,128]{1,0:T(8,128)(2,1)S(1)}, bf16[256,128]{1,0:T(8,128)(2,1)S(1)}, u32[]{:S(2)}, u32[]{:S(2)}) collective-permute-start(bf16[256,128]{1,0:T(8,128)(2,1)S(1)} %get-tuple-element.48), channel_id=1, source_target_pairs={{0,6},{1,7},{2,4},{3,5},{4,2},{5,3},{6,0},{7,1},{8,14},{9,15},{10,... | collective-permute-start | bytes 196616 | tf_op jit(solution)/shard_map/ppermute | solution.py:458
  57.2 1.6 %collective-permute-done.7.got_ref = bf16[4,256,128]{2,1,0:T(8,128)(2,1)S(1)} collective-permute-done((bf16[4,256,128]{2,1,0:T(8,128)(2,1)S(1)}, bf16[4,256,128]{2,1,0:T(8,128)(2,1)S(1)}, u32[]{:S(2)}, u32[]{:S(2)}) %collective-permute-start.7) | collective-permute-done | bytes 262176 | tf_op jit(solution)/shard_map/ppermute | solution.py:445
  58.8 0.1 pair_sums.3
  58.8 0.8 %collective-permute-start.10 = (bf16[256,128]{1,0:T(8,128)(2,1)S(1)}, bf16[256,128]{1,0:T(8,128)(2,1)S(1)}, u32[]{:S(2)}, u32[]{:S(2)}) collective-permute-start(bf16[256,128]{1,0:T(8,128)(2,1)S(1)} %get-tuple-element.55), channel_id=1, source_target_pairs={{0,6},{1,7},{2,4},{3,5},{4,2},{5,3},{6,0},{7,1},{8,14},{9,15},{10,... | collective-permute-start | bytes 196616 | tf_op jit(solution)/shard_map/ppermute | solution.py:458
  59.7 0.5 collective-permute-start.8
  60.2 0.0 collective-permute-done.4.refs_1_
  60.2 3.1 %collective-permute-start.9 = (bf16[256,128]{1,0:T(8,128)(2,1)S(1)}, bf16[256,128]{1,0:T(8,128)(2,1)S(1)}, u32[]{:S(2)}, u32[]{:S(2)}) collective-permute-start(bf16[256,128]{1,0:T(8,128)(2,1)S(1)} %get-tuple-element.54), channel_id=1, source_target_pairs={{0,4},{1,5},{2,6},{3,7},{4,0},{5,1},{6,2},{7,3},{8,12},{9,13},{10,... | collective-permute-start | bytes 196616 | tf_op jit(solution)/shard_map/ppermute | solution.py:458
  63.3 0.0 collective-permute-done.5.refs_2_
  63.3 0.0 collective-permute-done.6.refs_3_
  63.3 1.8 %collective-permute-done.10.refs_7_ = bf16[256,128]{1,0:T(8,128)(2,1)S(1)} collective-permute-done((bf16[256,128]{1,0:T(8,128)(2,1)S(1)}, bf16[256,128]{1,0:T(8,128)(2,1)S(1)}, u32[]{:S(2)}, u32[]{:S(2)}) %collective-permute-start.10) | collective-permute-done | bytes 65568 | tf_op jit(solution)/shard_map/ppermute | solution.py:458
  65.1 0.8 %collective-permute-done.8.refs_5_ = bf16[256,128]{1,0:T(8,128)(2,1)S(1)} collective-permute-done((bf16[256,128]{1,0:T(8,128)(2,1)S(1)}, bf16[256,128]{1,0:T(8,128)(2,1)S(1)}, u32[]{:S(2)}, u32[]{:S(2)}) %collective-permute-start.8) | collective-permute-done | bytes 65568 | tf_op jit(solution)/shard_map/ppermute | solution.py:458
  65.8 0.0 collective-permute-done.9.refs_6_
  65.9 0.7 %last_sums.1 = bf16[512,128]{1,0:T(8,128)(2,1)} custom-call(f32[256,128]{1,0:T(8,128)S(1)} %get-tuple-element.45.refs_0_, bf16[256,128]{1,0:T(8,128)(2,1)S(1)} %collective-permute-done.4.refs_1_, bf16[256,128]{1,0:T(8,128)(2,1)S(1)} %collective-permute-done.5.refs_2_, bf16[256,128]{1,0:T(8,128)(2,1)S(1)} %collective-permute-done.6.refs_3_, ...), custom_call_target="tpu_custom_call" | custom-call | tf_op jit(solution)/shard_map/last_sums/pallas_call | solution.py:459
Async XLA Ops:
  0.6 6.3 %copy-start.1 = (bf16[4,256,1024]{2,1,0:T(8,128)(2,1)S(1)}, bf16[4,256,1024]{2,1,0:T(8,128)(2,1)}, u32[]{:S(2)}) copy-start(bf16[4,256,1024]{2,1,0:T(8,128)(2,1)} %weights_ref.3) | copy-start | bytes 6291460
  0.6 6.3 %copy-start.2 = (s32[16,16]{1,0:T(8,128)S(1)}, s32[16,16]{1,0:T(8,128)}, u32[]{:S(2)}) copy-start(s32[16,16]{1,0:T(8,128)} %lists_hbm.1) | copy-start | bytes 3076
  0.7 6.3 %copy-start.4 = (s32[128]{0:T(128)S(1)}, s32[128]{0:T(128)}, u32[]{:S(2)}) copy-start(s32[128]{0:T(128)} %slot_hbm.1) | copy-start | bytes 1540
  0.7 7.9 %copy-start.3 = (s32[512,8]{0,1:T(8,128)S(1)}, s32[512,8]{0,1:T(8,128)}, u32[]{:S(2)}) copy-start(s32[512,8]{0,1:T(8,128)} %param.9) | copy-start | bytes 49156
  0.7 19.0 %copy-start = (bf16[512,1024]{1,0:T(8,128)(2,1)S(1)}, bf16[512,1024]{1,0:T(8,128)(2,1)}, u32[]{:S(2)}) copy-start(bf16[512,1024]{1,0:T(8,128)(2,1)} %param.5) | copy-start | bytes 3145732
  3.7 16.0 %collective-permute-start.2 = (bf16[256,1024]{1,0:T(8,128)(2,1)}, bf16[256,1024]{1,0:T(8,128)(2,1)S(1)}, u32[]{:S(2)}, u32[]{:S(2)}) collective-permute-start(bf16[256,1024]{1,0:T(8,128)(2,1)} %get-tuple-element.35), channel_id=1, source_target_pairs={{0,16},{8,24},{16,0},{24,8},{1,17},{9,25},{17,1},{25,9},{2,18},{10... | collective-permute-start | bytes 1572872 | tf_op jit(solution)/shard_map/ppermute | solution.py:343
  6.7 14.1 %collective-permute-start.1 = (bf16[256,1024]{1,0:T(8,128)(2,1)}, bf16[256,1024]{1,0:T(8,128)(2,1)S(1)}, u32[]{:S(2)}, u32[]{:S(2)}) collective-permute-start(bf16[256,1024]{1,0:T(8,128)(2,1)} %get-tuple-element.34), channel_id=1, source_target_pairs={{0,8},{8,0},{16,24},{24,16},{1,9},{9,1},{17,25},{25,17},{2,10},{10... | collective-permute-start | bytes 1572872 | tf_op jit(solution)/shard_map/ppermute | solution.py:343
  6.7 22.7 %collective-permute-start = (bf16[256,1024]{1,0:T(8,128)(2,1)}, bf16[256,1024]{1,0:T(8,128)(2,1)S(1)}, u32[]{:S(2)}, u32[]{:S(2)}) collective-permute-start(bf16[256,1024]{1,0:T(8,128)(2,1)} %get-tuple-element.32), channel_id=1, source_target_pairs={{0,24},{8,16},{16,8},{24,0},{1,25},{9,17},{17,9},{25,1},{2,26},{10... | collective-permute-start | bytes 1572872 | tf_op jit(solution)/shard_map/ppermute | solution.py:343
  44.7 7.5 %collective-permute-start.3 = (bf16[4,256,128]{2,1,0:T(8,128)(2,1)S(1)}, bf16[4,256,128]{2,1,0:T(8,128)(2,1)S(1)}, u32[]{:S(2)}, u32[]{:S(2)}) collective-permute-start(bf16[4,256,128]{2,1,0:T(8,128)(2,1)S(1)} %get-tuple-element.44), channel_id=1, source_target_pairs={{0,1},{1,0},{2,3},{3,2},{4,5},{5,4},{6,7},{7,6},{8,9},{9,8},{10,11... | collective-permute-start | bytes 786440 | tf_op jit(solution)/shard_map/ppermute | solution.py:445
  52.2 6.6 %collective-permute-start.7 = (bf16[4,256,128]{2,1,0:T(8,128)(2,1)S(1)}, bf16[4,256,128]{2,1,0:T(8,128)(2,1)S(1)}, u32[]{:S(2)}, u32[]{:S(2)}) collective-permute-start(bf16[4,256,128]{2,1,0:T(8,128)(2,1)S(1)} %get-tuple-element.51), channel_id=1, source_target_pairs={{0,1},{1,0},{2,3},{3,2},{4,5},{5,4},{6,7},{7,6},{8,9},{9,8},{10,11... | collective-permute-start | bytes 786440 | tf_op jit(solution)/shard_map/ppermute | solution.py:445
  52.7 7.5 %collective-permute-start.4 = (bf16[256,128]{1,0:T(8,128)(2,1)S(1)}, bf16[256,128]{1,0:T(8,128)(2,1)S(1)}, u32[]{:S(2)}, u32[]{:S(2)}) collective-permute-start(bf16[256,128]{1,0:T(8,128)(2,1)S(1)} %get-tuple-element.46), channel_id=1, source_target_pairs={{0,2},{1,3},{2,0},{3,1},{4,6},{5,7},{6,4},{7,5},{8,10},{9,11},{10,... | collective-permute-start | bytes 196616 | tf_op jit(solution)/shard_map/ppermute | solution.py:458
  53.5 9.8 %collective-permute-start.5 = (bf16[256,128]{1,0:T(8,128)(2,1)S(1)}, bf16[256,128]{1,0:T(8,128)(2,1)S(1)}, u32[]{:S(2)}, u32[]{:S(2)}) collective-permute-start(bf16[256,128]{1,0:T(8,128)(2,1)S(1)} %get-tuple-element.47), channel_id=1, source_target_pairs={{0,4},{1,5},{2,6},{3,7},{4,0},{5,1},{6,2},{7,3},{8,12},{9,13},{10,... | collective-permute-start | bytes 196616 | tf_op jit(solution)/shard_map/ppermute | solution.py:458
  54.5 8.8 %collective-permute-start.6 = (bf16[256,128]{1,0:T(8,128)(2,1)S(1)}, bf16[256,128]{1,0:T(8,128)(2,1)S(1)}, u32[]{:S(2)}, u32[]{:S(2)}) collective-permute-start(bf16[256,128]{1,0:T(8,128)(2,1)S(1)} %get-tuple-element.48), channel_id=1, source_target_pairs={{0,6},{1,7},{2,4},{3,5},{4,2},{5,3},{6,0},{7,1},{8,14},{9,15},{10,... | collective-permute-start | bytes 196616 | tf_op jit(solution)/shard_map/ppermute | solution.py:458
  58.8 6.2 %collective-permute-start.10 = (bf16[256,128]{1,0:T(8,128)(2,1)S(1)}, bf16[256,128]{1,0:T(8,128)(2,1)S(1)}, u32[]{:S(2)}, u32[]{:S(2)}) collective-permute-start(bf16[256,128]{1,0:T(8,128)(2,1)S(1)} %get-tuple-element.55), channel_id=1, source_target_pairs={{0,6},{1,7},{2,4},{3,5},{4,2},{5,3},{6,0},{7,1},{8,14},{9,15},{10,... | collective-permute-start | bytes 196616 | tf_op jit(solution)/shard_map/ppermute | solution.py:458
  59.7 6.2 %collective-permute-start.8 = (bf16[256,128]{1,0:T(8,128)(2,1)S(1)}, bf16[256,128]{1,0:T(8,128)(2,1)S(1)}, u32[]{:S(2)}, u32[]{:S(2)}) collective-permute-start(bf16[256,128]{1,0:T(8,128)(2,1)S(1)} %get-tuple-element.53), channel_id=1, source_target_pairs={{0,2},{1,3},{2,0},{3,1},{4,6},{5,7},{6,4},{7,5},{8,10},{9,11},{10,... | collective-permute-start | bytes 196616 | tf_op jit(solution)/shard_map/ppermute | solution.py:458
  60.2 5.6 %collective-permute-start.9 = (bf16[256,128]{1,0:T(8,128)(2,1)S(1)}, bf16[256,128]{1,0:T(8,128)(2,1)S(1)}, u32[]{:S(2)}, u32[]{:S(2)}) collective-permute-start(bf16[256,128]{1,0:T(8,128)(2,1)S(1)} %get-tuple-element.54), channel_id=1, source_target_pairs={{0,4},{1,5},{2,6},{3,7},{4,0},{5,1},{6,2},{7,3},{8,12},{9,13},{10,... | collective-permute-start | bytes 196616 | tf_op jit(solution)/shard_map/ppermute | solution.py:458

commit v2 on v1

--- a/solution.py
+++ b/solution.py
@@ -219,8 +219,9 @@
 
 def half_kernel(side, groups, lab_count, pos_count, table_ref, hits_ref, shares_ref, stats_ref, *rest):
     logits_refs = rest[: len(groups)]
-    rows = rest[len(groups) : -6]
-    loss_ref, keep_ref, send_ref, lse_ref, columns_ref, total_ref = rest[-6:]
+    dp_count = sum(len(slots) for slots in groups)
+    rows = rest[len(groups) : len(groups) + dp_count]
+    loss_ref, keep_ref, *send_refs, lse_ref, columns_ref, total_ref = rest[len(groups) + dp_count :]
     half = total_ref.shape[0]
     prepare(
         stats_ref, pos_count, lab_count, loss_ref, lse_ref, columns_ref, total_ref, side * half
@@ -239,29 +240,45 @@
     )
     part = keep_ref.shape[2]
     lab_index = lax.axis_index("label")
-    for j in range(lab_count // 2):
-        mine = pl.ds(pl.multiple_of((lab_index ^ (2 * j)) * part, part), part)
-        other = pl.ds(pl.multiple_of((lab_index ^ (2 * j + 1)) * part, part), part)
+
+    def cut(ref, i, offset):
+        features = pl.ds(pl.multiple_of((lab_index ^ offset) * part, part), part)
         for b in range(half):
-            here = pl.ds(b * BLK, BLK)
-            keep_ref[j, here, :] = total_ref[b, :, mine]
-            send_ref[j, here, :] = total_ref[b, :, other].astype(jnp.bfloat16)
+            ref[i, b * BLK : (b + 1) * BLK, :] = total_ref[b, :, features].astype(ref.dtype)
+
+    if side == 0:
+        for j in range(lab_count // 2):
+            cut(keep_ref, j, 2 * j)
+            cut(send_refs[0], j, 2 * j + 1)
+    else:
+        for x in range(2):
+            cut(keep_ref, x, x)
+            for j, ref in enumerate(send_refs):
+                cut(ref, x, 2 * j + 2 + x)
 
 
 def pair_kernel(keep_ref, got_ref, *outs):
-    outs[0][...] = keep_ref[0] + got_ref[0].astype(jnp.float32)
-    for j in range(1, len(outs)):
-        outs[j][...] = (keep_ref[j] + got_ref[j].astype(jnp.float32)).astype(jnp.bfloat16)
+    for j, out_ref in enumerate(outs):
+        out_ref[...] = (keep_ref[j] + got_ref[j].astype(jnp.float32)).astype(out_ref.dtype)
+
+
+def line_kernel(keep_ref, *refs):
+    for x, out_ref in enumerate(refs[-2:]):
+        total = keep_ref[x]
+        for ref in refs[:-2]:
+            total = total + ref[x].astype(jnp.float32)
+        out_ref[...] = total.astype(out_ref.dtype)
 
 
 def last_kernel(count, *refs):
     out_ref = refs[-1]
-    for h in range(len(refs[:-1]) // count):
-        total = refs[h * count][...]
-        for ref in refs[h * count + 1 : (h + 1) * count]:
+    at = 0
+    for parts in (refs[:count], refs[count:-1]):
+        total = parts[0][...]
+        for ref in parts[1:]:
             total = total + ref[...].astype(jnp.float32)
-        rows = total.shape[0]
-        out_ref[h * rows : (h + 1) * rows, :] = total.astype(jnp.bfloat16)
+        out_ref[at : at + total.shape[0], :] = total.astype(jnp.bfloat16)
+        at += total.shape[0]
 
 
 def grad_kernel(groups, lab_count, pos_count, table_ref, hits_ref, shares_ref, stats_ref, *rest):
@@ -416,54 +433,56 @@
 
     pairs = lab_count // 2
     half_rows = inst_count // 2
-    finals = []
-    for side in range(2):
-        loss, keep, send = pl.pallas_call(
+    wide = jax.ShapeDtypeStruct((half_rows, part), jnp.float32)
+    narrow = jax.ShapeDtypeStruct((half_rows, part), jnp.bfloat16)
+
+    def stack(count, one):
+        return jax.ShapeDtypeStruct((count,) + one.shape, one.dtype)
+
+    def swap(x, mask):
+        return lax.ppermute(x, "label", [(i, i ^ mask) for i in range(lab_count)])
+
+    def call(kernel, name, out_shape, *arrays):
+        return pl.pallas_call(
+            kernel,
+            out_shape=out_shape,
+            in_specs=[vmem()] * len(arrays),
+            out_specs=jax.tree.map(lambda _: vmem(), out_shape),
+            compiler_params=params,
+            name=name,
+        )(*arrays)
+
+    def half(side, outs):
+        return pl.pallas_call(
             functools.partial(half_kernel, side, groups, lab_count, pos_count),
-            out_shape=[
-                loss_type,
-                jax.ShapeDtypeStruct((pairs, half_rows, part), jnp.float32),
-                jax.ShapeDtypeStruct((pairs, half_rows, part), jnp.bfloat16),
-            ],
+            out_shape=[loss_type] + outs,
             in_specs=in_specs,
-            out_specs=[vmem()] * 3,
+            out_specs=[vmem()] * (1 + len(outs)),
             scratch_shapes=[
                 lse_scratch,
                 pltpu.VMEM((block_count // 2, BLK, BLK), jnp.float32),
                 pltpu.VMEM((block_count // 2, BLK, width), jnp.float32),
             ],
             compiler_params=params,
-            cost_estimate=pl.CostEstimate(
-                flops=dp_count * 2 * BLK * cluster_size * width,
-                bytes_accessed=dp_count * cluster_size * width * 2,
-                transcendentals=0,
-            ),
             name="grads",
         )(*operands)
-        if side:
-            send, got = lax.optimization_barrier((send, got))
-        got = lax.ppermute(send, "label", [(i, i ^ 1) for i in range(lab_count)])
-        own, *outgoing = pl.pallas_call(
-            pair_kernel,
-            out_shape=[jax.ShapeDtypeStruct((half_rows, part), jnp.float32)]
-            + [jax.ShapeDtypeStruct((half_rows, part), jnp.bfloat16)] * (pairs - 1),
-            in_specs=[vmem()] * 2,
-            out_specs=[vmem()] * pairs,
-            compiler_params=params,
-            name="pair_sums",
-        )(keep, got)
-        finals.append(own)
-        for j in range(1, pairs):
-            hop = [(i, i ^ (2 * j)) for i in range(lab_count)]
-            finals.append(lax.ppermute(outgoing[j - 1], "label", hop))
-    grads = pl.pallas_call(
-        functools.partial(last_kernel, pairs),
-        out_shape=jax.ShapeDtypeStruct((inst_count, part), jnp.bfloat16),
-        in_specs=[vmem()] * (2 * pairs),
-        out_specs=vmem(),
-        compiler_params=params,
-        name="last_sums",
-    )(*finals)
+
+    loss, keep, send = half(0, [stack(pairs, wide), stack(pairs, narrow)])
+    got = swap(send, 1)
+    _, line_keep, *line_send = half(1, [stack(2, wide)] + [stack(2, narrow)] * (pairs - 1))
+    line_got = [swap(x, 2 * j + 2) for j, x in enumerate(line_send)]
+    own, *sends = call(pair_kernel, "pair_sums", [wide] + [narrow] * (pairs - 1), keep, got)
+    line_keep, *sends = lax.optimization_barrier((line_keep, *sends))
+    first = [own] + [swap(x, 2 * j + 2) for j, x in enumerate(sends)]
+    line_own, line_out = call(line_kernel, "line_sums", [wide, narrow], line_keep, *line_got)
+    second = [line_own, swap(line_out, 1)]
+    grads = call(
+        functools.partial(last_kernel, len(first)),
+        "last_sums",
+        jax.ShapeDtypeStruct((inst_count, part), jnp.bfloat16),
+        *first,
+        *second,
+    )
     return loss.reshape(inst_count), grads
 
 

time: 66.8 us -> 68.3 us (1.022)
  starting transfers between devices: 13 us -> 13.9 us
    ppermute x8, starting transfers between devices: 9.77 us -> 10.7 us  [swap(): return lax.ppermute(x, 'label', [(i, i ^ mask) for i in range(lab_count)])]
where the time goes in v2:
time: 68.3 us; the launch traced here: 67.8 us
  waiting for transfers between devices  26.3 us (39%)
  Pallas kernels  14.4 us (21%)
  starting transfers between devices  13.9 us (20%)
  blocking collectives  12.4 us (18%)
  between operations  0.73 us (1%)
    ppermute x3, waiting for transfers between devices, shards(): rows[k] = lax.ppermute(rows[k], 'dp', [(i, i ^ k) for i in range(dp_count)])  16.6 us
    all_to_all x1, blocking collectives, shards(): lax.all_to_all(stats[0], 'label', split_axis=0, concat_axis=0, tiled=True)  12.4 us
    ppermute x8, starting transfers between devices, swap(): return lax.ppermute(x, 'label', [(i, i ^ mask) for i in range(lab_count)])  10.7 us
    ppermute x8, waiting for transfers between devices, swap(): return lax.ppermute(x, 'label', [(i, i ^ mask) for i in range(lab_count)])  9.74 us
    pallas_call x2, Pallas kernels, half(): pl.pallas_call(functools.partial(half_kernel, side, groups, lab_count, po...  3.6 us
    pallas_call x3, Pallas kernels, shards(): pl.pallas_call(functools.partial(logit_kernel, slots, not last, copies),...  3.58 us
    ppermute x3, starting transfers between devices, shards(): rows[k] = lax.ppermute(rows[k], 'dp', [(i, i ^ k) for i in range(dp_count)])  3.24 us
    pallas_call x1, Pallas kernels, shards(): pl.pallas_call(functools.partial(far_kernel, sizes, far), out_shape=[row_...  2.97 us
  transfers between devices with their start and end apart: 11, of which 6 were waited for; matrix products, arithmetic and copies ran while one was open for 0% of the time, Pallas kernels for 12%

profile of v2, /device:TPU:0, one launch (start us, length us, event | category | flops | bytes accessed | tf_op | source)
XLA Modules:
  0.0 67.8 jit_solution(6259619966391732949)
XLA Ops:
  0.6 0.0 copy-start.2
  0.6 0.0 copy-start.4
  0.7 0.0 copy-start.1
  0.7 0.0 copy-start.3
  0.7 0.0 copy-start
  0.7 3.0 %pick_far.1 = (bf16[256,1024]{1,0:T(8,128)(2,1)}, bf16[256,1024]{1,0:T(8,128)(2,1)}, bf16[256,1024]{1,0:T(8,128)(2,1)}) custom-call(s32[16,16]{1,0:T(8,128)} %lists_hbm.1, s32[128]{0:T(128)} %slot_hbm.1, bf16[4,256,1024]{2,1,0:T(8,128)(2,1)} %weights_ref.3), custom_call_target="tpu_custom_call" | custom-call | tf_op jit(solution)/shard_map/pick_far/pallas_call | solution.py:335
  3.7 3.0 %collective-permute-start.2 = (bf16[256,1024]{1,0:T(8,128)(2,1)}, bf16[256,1024]{1,0:T(8,128)(2,1)S(1)}, u32[]{:S(2)}, u32[]{:S(2)}) collective-permute-start(bf16[256,1024]{1,0:T(8,128)(2,1)} %get-tuple-element.38), channel_id=1, source_target_pairs={{0,16},{8,24},{16,0},{24,8},{1,17},{9,25},{17,1},{25,9},{2,18},{10... | collective-permute-start | bytes 1572872 | tf_op jit(solution)/shard_map/ppermute | solution.py:360
  6.7 0.0 collective-permute-start.1
  6.7 0.2 collective-permute-start
  6.9 0.0 copy-done.2
  6.9 0.0 copy-done.4
  6.9 0.0 copy-done.1
  6.9 1.6 %pick_near.1 = (s32[4,4]{1,0:T(4,128)S(1)}, bf16[256,1024]{1,0:T(8,128)(2,1)S(1)}) custom-call(s32[16,16]{1,0:T(8,128)S(1)} %copy-done.2, s32[128]{0:T(128)S(1)} %copy-done.4, bf16[4,256,1024]{2,1,0:T(8,128)(2,1)S(1)} %copy-done.1), custom_call_target="tpu_custom_call" | custom-call | tf_op jit(solution)/shard_map/pick_near/pallas_call | solution.py:349
  8.6 0.0 copy-done.3
  8.6 1.7 %targets.1 = (f32[4,256,256]{2,1,0:T(8,128)S(1)}, f32[3,256,256]{2,1,0:T(8,128)S(1)}) custom-call(s32[4,4]{1,0:T(4,128)S(1)} %get-tuple-element.32.table_ref, s32[4,8,128]{2,1,0:T(8,128)S(1)} %bitcast.8), custom_call_target="tpu_custom_call" | custom-call | tf_op jit(solution)/shard_map/targets/pallas_call | solution.py:369
  10.3 9.3 %collective-permute-done.2.rest_0_.rest_5_ = bf16[256,1024]{1,0:T(8,128)(2,1)S(1)} collective-permute-done((bf16[256,1024]{1,0:T(8,128)(2,1)}, bf16[256,1024]{1,0:T(8,128)(2,1)S(1)}, u32[]{:S(2)}, u32[]{:S(2)}) %collective-permute-start.2) | collective-permute-done | bytes 524320 | tf_op jit(solution)/shard_map/ppermute | solution.py:360
  19.6 0.0 copy-done
  19.7 1.1 %logits.3 = (f32[1,256,256]{2,1,0:T(8,128)S(1)}, f32[1,3,4,128]{3,2,1,0:T(4,128)S(1)}) custom-call(s32[4,4]{1,0:T(4,128)S(1)} %get-tuple-element.32.table_ref, bf16[4,128,1024]{2,1,0:T(8,128)(2,1)S(1)} %bitcast.5, f32[4,256,256]{2,1,0:T(8,128)S(1)} %get-tuple-element.33.hits_ref, bf16[256,1024]{1,0:T(8,128)(2,1)S(1)} %collective-permute-done.2.rest_0_.rest_5_), custom_call_target="tpu_custom_call" | custom-call | flops 134217728 | bytes 524288 | tf_op jit(solution)/shard_map/logits/pallas_call | solution.py:387
  20.8 0.0 collective-permute-done.1.rest_1_.rest_4_
  20.8 1.4 %logits.4 = (f32[2,256,256]{2,1,0:T(8,128)S(1)}, f32[1,3,4,128]{3,2,1,0:T(4,128)S(1)}) custom-call(s32[4,4]{1,0:T(4,128)S(1)} %get-tuple-element.32.table_ref, bf16[4,128,1024]{2,1,0:T(8,128)(2,1)S(1)} %bitcast.6, f32[4,256,256]{2,1,0:T(8,128)S(1)} %get-tuple-element.33.hits_ref, bf16[256,1024]{1,0:T(8,128)(2,1)S(1)} %get-tuple-element.36.rest_0_.rest_3_, ...), custom_call_target="tpu_custom_call" | custom-call | flops 268435456 | bytes 1048576 | tf_op jit(solution)/shard_map/logits/pallas_call | solution.py:387
  22.2 7.3 %collective-permute-done.rest_0_.rest_6_ = bf16[256,1024]{1,0:T(8,128)(2,1)S(1)} collective-permute-done((bf16[256,1024]{1,0:T(8,128)(2,1)}, bf16[256,1024]{1,0:T(8,128)(2,1)S(1)}, u32[]{:S(2)}, u32[]{:S(2)}) %collective-permute-start) | collective-permute-done | bytes 524320 | tf_op jit(solution)/shard_map/ppermute | solution.py:360
  29.4 1.1 %logits.5 = (f32[1,256,256]{2,1,0:T(8,128)S(1)}, f32[8,3,4,128]{3,2,1,0:T(4,128)S(1)}) custom-call(s32[4,4]{1,0:T(4,128)S(1)} %get-tuple-element.32.table_ref, bf16[4,128,1024]{2,1,0:T(8,128)(2,1)S(1)} %bitcast.7, f32[4,256,256]{2,1,0:T(8,128)S(1)} %get-tuple-element.33.hits_ref, bf16[256,1024]{1,0:T(8,128)(2,1)S(1)} %collective-permute-done.rest_0_.rest_6_, ...), custom_call_target="tpu_custom_call" | custom-call | flops 134217728 | bytes 524288 | tf_op jit(solution)/shard_map/logits/pallas_call | solution.py:387
  30.5 12.4 %all_to_all.5.stats_ref = f32[8,3,4,128]{3,2,1,0:T(4,128)S(1)} all-to-all(f32[8,3,4,128]{3,2,1,0:T(4,128)S(1)} %get-tuple-element.41), channel_id=1, replica_groups=mesh['dp'=4,'label'=8] {'label'}, dimensions={0} | all-to-all | bytes 98304 | tf_op jit(solution)/shard_map/all_to_all | solution.py:407
  42.9 1.8 %grads.2 = (f32[4,128]{1,0:T(4,128)}, f32[4,256,128]{2,1,0:T(8,128)S(1)}, bf16[4,256,128]{2,1,0:T(8,128)(2,1)S(1)}) custom-call(s32[4,4]{1,0:T(4,128)S(1)} %get-tuple-element.32.table_ref, f32[4,256,256]{2,1,0:T(8,128)S(1)} %get-tuple-element.33.hits_ref, f32[3,256,256]{2,1,0:T(8,128)S(1)} %get-tuple-element.34.shares_ref, ...), custom_call_target="tpu_custom_call" | custom-call | tf_op jit(solution)/shard_map/grads/pallas_call | solution.py:456
  44.7 0.4 collective-permute-start.3
  45.1 1.8 %grads.3 = (f32[4,128]{1,0:T(4,128)}, f32[2,256,128]{2,1,0:T(8,128)S(1)}, bf16[2,256,128]{2,1,0:T(8,128)(2,1)S(1)}, bf16[2,256,128]{2,1,0:T(8,128)(2,1)S(1)}, bf16[2,256,128]{2,1,0:T(8,128)(2,1)S(1)}) custom-call(s32[4,4]{1,0:T(4,128)S(1)} %get-tuple-element.32.table_ref, f32[4,256,256]{2,1,0:T(8,128)S(1)} %get-tuple-element.33.hits_ref, ...), custom_call_target="tpu_custom_call" | custom-call | tf_op jit(solution)/shard_map/grads/pallas_call | solution.py:456
  46.9 0.8 %collective-permute-start.7 = (bf16[2,256,128]{2,1,0:T(8,128)(2,1)S(1)}, bf16[2,256,128]{2,1,0:T(8,128)(2,1)S(1)}, u32[]{:S(2)}, u32[]{:S(2)}) collective-permute-start(bf16[2,256,128]{2,1,0:T(8,128)(2,1)S(1)} %get-tuple-element.57), channel_id=1, source_target_pairs={{0,2},{1,3},{2,0},{3,1},{4,6},{5,7},{6,4},{7,5},{8,10},{9,11},{10,... | collective-permute-start | bytes 393224 | tf_op jit(solution)/shard_map/ppermute | solution.py:443
  47.7 0.7 %collective-permute-start.8 = (bf16[2,256,128]{2,1,0:T(8,128)(2,1)S(1)}, bf16[2,256,128]{2,1,0:T(8,128)(2,1)S(1)}, u32[]{:S(2)}, u32[]{:S(2)}) collective-permute-start(bf16[2,256,128]{2,1,0:T(8,128)(2,1)S(1)} %get-tuple-element.58), channel_id=1, source_target_pairs={{0,4},{1,5},{2,6},{3,7},{4,0},{5,1},{6,2},{7,3},{8,12},{9,13},{10,... | collective-permute-start | bytes 393224 | tf_op jit(solution)/shard_map/ppermute | solution.py:443
  48.4 2.9 %collective-permute-start.9 = (bf16[2,256,128]{2,1,0:T(8,128)(2,1)S(1)}, bf16[2,256,128]{2,1,0:T(8,128)(2,1)S(1)}, u32[]{:S(2)}, u32[]{:S(2)}) collective-permute-start(bf16[2,256,128]{2,1,0:T(8,128)(2,1)S(1)} %get-tuple-element.59), channel_id=1, source_target_pairs={{0,6},{1,7},{2,4},{3,5},{4,2},{5,3},{6,0},{7,1},{8,14},{9,15},{10,... | collective-permute-start | bytes 393224 | tf_op jit(solution)/shard_map/ppermute | solution.py:443
  51.3 0.9 %collective-permute-done.3.got_ref = bf16[4,256,128]{2,1,0:T(8,128)(2,1)S(1)} collective-permute-done((bf16[4,256,128]{2,1,0:T(8,128)(2,1)S(1)}, bf16[4,256,128]{2,1,0:T(8,128)(2,1)S(1)}, u32[]{:S(2)}, u32[]{:S(2)}) %collective-permute-start.3) | collective-permute-done | bytes 262176 | tf_op jit(solution)/shard_map/ppermute | solution.py:443
  52.2 0.1 pair_sums.1
  52.3 0.4 collective-permute-start.4
  52.6 0.9 %collective-permute-start.5 = (bf16[256,128]{1,0:T(8,128)(2,1)S(1)}, bf16[256,128]{1,0:T(8,128)(2,1)S(1)}, u32[]{:S(2)}, u32[]{:S(2)}) collective-permute-start(bf16[256,128]{1,0:T(8,128)(2,1)S(1)} %get-tuple-element.54), channel_id=1, source_target_pairs={{0,4},{1,5},{2,6},{3,7},{4,0},{5,1},{6,2},{7,3},{8,12},{9,13},{10,... | collective-permute-start | bytes 196616 | tf_op jit(solution)/shard_map/ppermute | solution.py:443
  53.6 0.0 collective-permute-done.7.refs_0_
  53.6 3.1 %collective-permute-start.6 = (bf16[256,128]{1,0:T(8,128)(2,1)S(1)}, bf16[256,128]{1,0:T(8,128)(2,1)S(1)}, u32[]{:S(2)}, u32[]{:S(2)}) collective-permute-start(bf16[256,128]{1,0:T(8,128)(2,1)S(1)} %get-tuple-element.55), channel_id=1, source_target_pairs={{0,6},{1,7},{2,4},{3,5},{4,2},{5,3},{6,0},{7,1},{8,14},{9,15},{10,... | collective-permute-start | bytes 196616 | tf_op jit(solution)/shard_map/ppermute | solution.py:443
  56.7 6.0 %collective-permute-done.8.refs_1_ = bf16[2,256,128]{2,1,0:T(8,128)(2,1)S(1)} collective-permute-done((bf16[2,256,128]{2,1,0:T(8,128)(2,1)S(1)}, bf16[2,256,128]{2,1,0:T(8,128)(2,1)S(1)}, u32[]{:S(2)}, u32[]{:S(2)}) %collective-permute-start.8) | collective-permute-done | bytes 131104 | tf_op jit(solution)/shard_map/ppermute | solution.py:443
  62.7 0.0 collective-permute-done.9.refs_2_
  62.7 0.1 line_sums.1
  62.8 1.4 %collective-permute-start.10 = (bf16[256,128]{1,0:T(8,128)(2,1)S(1)}, bf16[256,128]{1,0:T(8,128)(2,1)S(1)}, u32[]{:S(2)}, u32[]{:S(2)}) collective-permute-start(bf16[256,128]{1,0:T(8,128)(2,1)S(1)} %get-tuple-element.61), channel_id=1, source_target_pairs={{0,1},{1,0},{2,3},{3,2},{4,5},{5,4},{6,7},{7,6},{8,9},{9,8},{10,11... | collective-permute-start | bytes 196616 | tf_op jit(solution)/shard_map/ppermute | solution.py:443
  64.2 0.0 collective-permute-done.4.refs_1_
  64.2 1.9 %collective-permute-done.5.refs_2_ = bf16[256,128]{1,0:T(8,128)(2,1)S(1)} collective-permute-done((bf16[256,128]{1,0:T(8,128)(2,1)S(1)}, bf16[256,128]{1,0:T(8,128)(2,1)S(1)}, u32[]{:S(2)}, u32[]{:S(2)}) %collective-permute-start.5) | collective-permute-done | bytes 65568 | tf_op jit(solution)/shard_map/ppermute | solution.py:443
  66.1 0.0 collective-permute-done.6.refs_3_
  66.1 1.0 %collective-permute-done.10.refs_5_ = bf16[256,128]{1,0:T(8,128)(2,1)S(1)} collective-permute-done((bf16[256,128]{1,0:T(8,128)(2,1)S(1)}, bf16[256,128]{1,0:T(8,128)(2,1)S(1)}, u32[]{:S(2)}, u32[]{:S(2)}) %collective-permute-start.10) | collective-permute-done | bytes 65568 | tf_op jit(solution)/shard_map/ppermute | solution.py:443
  67.1 0.7 %last_sums.1 = bf16[512,128]{1,0:T(8,128)(2,1)} custom-call(f32[256,128]{1,0:T(8,128)S(1)} %get-tuple-element.48.refs_0_, bf16[256,128]{1,0:T(8,128)(2,1)S(1)} %collective-permute-done.4.refs_1_, bf16[256,128]{1,0:T(8,128)(2,1)S(1)} %collective-permute-done.5.refs_2_, bf16[256,128]{1,0:T(8,128)(2,1)S(1)} %collective-permute-done.6.refs_3_, ...), custom_call_target="tpu_custom_call" | custom-call | tf_op jit(solution)/shard_map/last_sums/pallas_call | solution.py:446
Async XLA Ops:
  0.6 6.3 %copy-start.2 = (s32[16,16]{1,0:T(8,128)S(1)}, s32[16,16]{1,0:T(8,128)}, u32[]{:S(2)}) copy-start(s32[16,16]{1,0:T(8,128)} %lists_hbm.1) | copy-start | bytes 3076
  0.6 6.3 %copy-start.4 = (s32[128]{0:T(128)S(1)}, s32[128]{0:T(128)}, u32[]{:S(2)}) copy-start(s32[128]{0:T(128)} %slot_hbm.1) | copy-start | bytes 1540
  0.7 6.3 %copy-start.1 = (bf16[4,256,1024]{2,1,0:T(8,128)(2,1)S(1)}, bf16[4,256,1024]{2,1,0:T(8,128)(2,1)}, u32[]{:S(2)}) copy-start(bf16[4,256,1024]{2,1,0:T(8,128)(2,1)} %weights_ref.3) | copy-start | bytes 6291460
  0.7 7.9 %copy-start.3 = (s32[512,8]{0,1:T(8,128)S(1)}, s32[512,8]{0,1:T(8,128)}, u32[]{:S(2)}) copy-start(s32[512,8]{0,1:T(8,128)} %param.9) | copy-start | bytes 49156
  0.7 19.0 %copy-start = (bf16[512,1024]{1,0:T(8,128)(2,1)S(1)}, bf16[512,1024]{1,0:T(8,128)(2,1)}, u32[]{:S(2)}) copy-start(bf16[512,1024]{1,0:T(8,128)(2,1)} %param.5) | copy-start | bytes 3145732
  3.7 16.0 %collective-permute-start.2 = (bf16[256,1024]{1,0:T(8,128)(2,1)}, bf16[256,1024]{1,0:T(8,128)(2,1)S(1)}, u32[]{:S(2)}, u32[]{:S(2)}) collective-permute-start(bf16[256,1024]{1,0:T(8,128)(2,1)} %get-tuple-element.38), channel_id=1, source_target_pairs={{0,16},{8,24},{16,0},{24,8},{1,17},{9,25},{17,1},{25,9},{2,18},{10... | collective-permute-start | bytes 1572872 | tf_op jit(solution)/shard_map/ppermute | solution.py:360
  6.7 14.1 %collective-permute-start.1 = (bf16[256,1024]{1,0:T(8,128)(2,1)}, bf16[256,1024]{1,0:T(8,128)(2,1)S(1)}, u32[]{:S(2)}, u32[]{:S(2)}) collective-permute-start(bf16[256,1024]{1,0:T(8,128)(2,1)} %get-tuple-element.37), channel_id=1, source_target_pairs={{0,8},{8,0},{16,24},{24,16},{1,9},{9,1},{17,25},{25,17},{2,10},{10... | collective-permute-start | bytes 1572872 | tf_op jit(solution)/shard_map/ppermute | solution.py:360
  6.7 22.7 %collective-permute-start = (bf16[256,1024]{1,0:T(8,128)(2,1)}, bf16[256,1024]{1,0:T(8,128)(2,1)S(1)}, u32[]{:S(2)}, u32[]{:S(2)}) collective-permute-start(bf16[256,1024]{1,0:T(8,128)(2,1)} %get-tuple-element.35), channel_id=1, source_target_pairs={{0,24},{8,16},{16,8},{24,0},{1,25},{9,17},{17,9},{25,1},{2,26},{10... | collective-permute-start | bytes 1572872 | tf_op jit(solution)/shard_map/ppermute | solution.py:360
  44.7 7.5 %collective-permute-start.3 = (bf16[4,256,128]{2,1,0:T(8,128)(2,1)S(1)}, bf16[4,256,128]{2,1,0:T(8,128)(2,1)S(1)}, u32[]{:S(2)}, u32[]{:S(2)}) collective-permute-start(bf16[4,256,128]{2,1,0:T(8,128)(2,1)S(1)} %get-tuple-element.47), channel_id=1, source_target_pairs={{0,1},{1,0},{2,3},{3,2},{4,5},{5,4},{6,7},{7,6},{8,9},{9,8},{10,11... | collective-permute-start | bytes 786440 | tf_op jit(solution)/shard_map/ppermute | solution.py:443
  46.9 6.6 %collective-permute-start.7 = (bf16[2,256,128]{2,1,0:T(8,128)(2,1)S(1)}, bf16[2,256,128]{2,1,0:T(8,128)(2,1)S(1)}, u32[]{:S(2)}, u32[]{:S(2)}) collective-permute-start(bf16[2,256,128]{2,1,0:T(8,128)(2,1)S(1)} %get-tuple-element.57), channel_id=1, source_target_pairs={{0,2},{1,3},{2,0},{3,1},{4,6},{5,7},{6,4},{7,5},{8,10},{9,11},{10,... | collective-permute-start | bytes 393224 | tf_op jit(solution)/shard_map/ppermute | solution.py:443
  47.7 15.0 %collective-permute-start.8 = (bf16[2,256,128]{2,1,0:T(8,128)(2,1)S(1)}, bf16[2,256,128]{2,1,0:T(8,128)(2,1)S(1)}, u32[]{:S(2)}, u32[]{:S(2)}) collective-permute-start(bf16[2,256,128]{2,1,0:T(8,128)(2,1)S(1)} %get-tuple-element.58), channel_id=1, source_target_pairs={{0,4},{1,5},{2,6},{3,7},{4,0},{5,1},{6,2},{7,3},{8,12},{9,13},{10,... | collective-permute-start | bytes 393224 | tf_op jit(solution)/shard_map/ppermute | solution.py:443
  48.4 14.3 %collective-permute-start.9 = (bf16[2,256,128]{2,1,0:T(8,128)(2,1)S(1)}, bf16[2,256,128]{2,1,0:T(8,128)(2,1)S(1)}, u32[]{:S(2)}, u32[]{:S(2)}) collective-permute-start(bf16[2,256,128]{2,1,0:T(8,128)(2,1)S(1)} %get-tuple-element.59), channel_id=1, source_target_pairs={{0,6},{1,7},{2,4},{3,5},{4,2},{5,3},{6,0},{7,1},{8,14},{9,15},{10,... | collective-permute-start | bytes 393224 | tf_op jit(solution)/shard_map/ppermute | solution.py:443
  52.3 11.9 %collective-permute-start.4 = (bf16[256,128]{1,0:T(8,128)(2,1)S(1)}, bf16[256,128]{1,0:T(8,128)(2,1)S(1)}, u32[]{:S(2)}, u32[]{:S(2)}) collective-permute-start(bf16[256,128]{1,0:T(8,128)(2,1)S(1)} %get-tuple-element.53), channel_id=1, source_target_pairs={{0,2},{1,3},{2,0},{3,1},{4,6},{5,7},{6,4},{7,5},{8,10},{9,11},{10,... | collective-permute-start | bytes 196616 | tf_op jit(solution)/shard_map/ppermute | solution.py:443
  52.6 13.4 %collective-permute-start.5 = (bf16[256,128]{1,0:T(8,128)(2,1)S(1)}, bf16[256,128]{1,0:T(8,128)(2,1)S(1)}, u32[]{:S(2)}, u32[]{:S(2)}) collective-permute-start(bf16[256,128]{1,0:T(8,128)(2,1)S(1)} %get-tuple-element.54), channel_id=1, source_target_pairs={{0,4},{1,5},{2,6},{3,7},{4,0},{5,1},{6,2},{7,3},{8,12},{9,13},{10,... | collective-permute-start | bytes 196616 | tf_op jit(solution)/shard_map/ppermute | solution.py:443
  53.6 12.5 %collective-permute-start.6 = (bf16[256,128]{1,0:T(8,128)(2,1)S(1)}, bf16[256,128]{1,0:T(8,128)(2,1)S(1)}, u32[]{:S(2)}, u32[]{:S(2)}) collective-permute-start(bf16[256,128]{1,0:T(8,128)(2,1)S(1)} %get-tuple-element.55), channel_id=1, source_target_pairs={{0,6},{1,7},{2,4},{3,5},{4,2},{5,3},{6,0},{7,1},{8,14},{9,15},{10,... | collective-permute-start | bytes 196616 | tf_op jit(solution)/shard_map/ppermute | solution.py:443
  62.8 4.3 %collective-permute-start.10 = (bf16[256,128]{1,0:T(8,128)(2,1)S(1)}, bf16[256,128]{1,0:T(8,128)(2,1)S(1)}, u32[]{:S(2)}, u32[]{:S(2)}) collective-permute-start(bf16[256,128]{1,0:T(8,128)(2,1)S(1)} %get-tuple-element.61), channel_id=1, source_target_pairs={{0,1},{1,0},{2,3},{3,2},{4,5},{5,4},{6,7},{7,6},{8,9},{9,8},{10,11... | collective-permute-start | bytes 196616 | tf_op jit(solution)/shard_map/ppermute | solution.py:443

commit v3 on v1

--- a/solution.py
+++ b/solution.py
@@ -74,13 +74,19 @@
         copy.wait()
 
 
-def near_kernel(sizes, lists_ref, slot_ref, weights_ref, table_ref, *rest):
+def near_kernel(sizes, lists_hbm, slot_hbm, weights_ref, table_ref, row_ref, lists_ref, slot_ref, sems):
     lab_count, stored, block_count, short_count = sizes
-    outs, sems = rest[:-1], rest[-1]
-    copies = []
-    for k, slot in enumerate(find_slots(sizes, range(1), lists_ref, slot_ref)):
-        copies.append(pltpu.make_async_copy(weights_ref.at[slot], outs[k], sems.at[k]))
-        copies[-1].start()
+    tables = [
+        pltpu.make_async_copy(lists_hbm, lists_ref, sems.at[0]),
+        pltpu.make_async_copy(slot_hbm, slot_ref, sems.at[1]),
+    ]
+    for copy in tables:
+        copy.start()
+    for copy in tables:
+        copy.wait()
+    (slot,) = find_slots(sizes, range(1), lists_ref, slot_ref)
+    own = pltpu.make_async_copy(weights_ref.at[slot], row_ref, sems.at[2])
+    own.start()
     dp_index, lab_index = lax.axis_index("dp"), lax.axis_index("label")
     half = block_count // 2
     for side in range(2):
@@ -99,8 +105,35 @@
             return carry
 
         each_entry(half * short_count, short_count, note, jnp.int32(0))
-    for copy in copies:
-        copy.wait()
+    own.wait()
+
+
+def before_kernel(sizes, early, lists, slots, weights, pos, *rest):
+    table, row, hits, shares, lists_ref, slot_ref, sems = rest[2:]
+
+    @pl.when((lax.axis_index("dp") & 1) == 1)
+    def _():
+        near_kernel(sizes, lists, slots, weights, table, row, lists_ref, slot_ref, sems)
+        target_kernel(early, table, pos, hits, shares)
+
+
+def after_kernel(sizes, early, lists, slots, weights, pos, *rest):
+    done, (table, row, hits, shares, lists_ref, slot_ref, sems) = rest[:4], rest[4:]
+    core = lax.axis_index("dp") & 1
+
+    @pl.when(core == 0)
+    def _():
+        near_kernel(sizes, lists, slots, weights, table, row, lists_ref, slot_ref, sems)
+        target_kernel(early, table, pos, hits, shares)
+
+    @pl.when(core == 1)
+    def _():
+        for i in range(table.shape[0]):
+            for j in range(table.shape[1] - 1):
+                table[i, j] = done[0][i, j]
+        row[...] = done[1][...]
+        hits[...] = done[2][...]
+        shares[...] = done[3][...]
 
 
 def target_kernel(early, table_ref, pos_ref, hits_ref, shares_ref):
@@ -329,37 +362,53 @@
         compiler_params=pltpu.CompilerParams(vmem_limit_bytes=VMEM_PICK),
         name="pick_far",
     )(shortlist, slot_of, weights)
-    table, *rows = pl.pallas_call(
-        functools.partial(near_kernel, sizes),
-        out_shape=[jax.ShapeDtypeStruct((dp_count, 4), jnp.int32)] + [row_type],
-        in_specs=[smem(), smem(), anywhere()],
-        out_specs=[smem(), vmem()],
-        scratch_shapes=[pltpu.SemaphoreType.DMA((1,))],
-        compiler_params=params,
-        name="pick_near",
-    )(shortlist, slot_of, weights)
-    rows += far_rows
-    for k in range(1, dp_count):
-        rows[k] = lax.ppermute(rows[k], "dp", [(i, i ^ k) for i in range(dp_count)])
-
-    feat_blocks = feats.reshape(block_count, BLK, width)
     pos_blocks = positives.reshape(block_count, BLK, pos_count).transpose(0, 2, 1)
     cuts = (0, dp_count // 2, dp_count * 3 // 4, dp_count)
     groups = [tuple(range(a, b)) for a, b in zip(cuts[:-1], cuts[1:])]
     if dp_count == 4:
         groups = [(2,), (0, 1), (3,)]
     early = [s for slots in groups[:-1] for s in slots]
-    hits, shares = pl.pallas_call(
-        functools.partial(target_kernel, early),
-        out_shape=[
-            jax.ShapeDtypeStruct((dp_count, cluster_size, 2 * BLK), jnp.float32),
-            jax.ShapeDtypeStruct((len(early), 2 * BLK, cluster_size), jnp.float32),
-        ],
-        in_specs=[smem(), vmem()],
-        out_specs=[vmem()] * 2,
+    near_types = [
+        jax.ShapeDtypeStruct((dp_count, 4), jnp.int32),
+        row_type,
+        jax.ShapeDtypeStruct((dp_count, cluster_size, 2 * BLK), jnp.float32),
+        jax.ShapeDtypeStruct((len(early), 2 * BLK, cluster_size), jnp.float32),
+    ]
+    near_operands = (shortlist, slot_of, weights, pos_blocks)
+    near_specs = [anywhere()] * 3 + [vmem()]
+    near_scratch = [
+        pltpu.SMEM(shortlist.shape, jnp.int32),
+        pltpu.SMEM(slot_of.shape, jnp.int32),
+        pltpu.SemaphoreType.DMA((3,)),
+    ]
+
+    def swap_dp(x, mask):
+        return lax.ppermute(x, "dp", [(i, i ^ mask) for i in range(dp_count)])
+
+    handed = [swap_dp(x, 1) if k % 2 == 0 and k else x for k, x in enumerate(far_rows)]
+    *sent, table, row, hits, shares = pl.pallas_call(
+        functools.partial(before_kernel, sizes, early),
+        out_shape=[row_type] + near_types,
+        in_specs=near_specs + [anywhere()],
+        out_specs=[anywhere(), smem()] + [vmem()] * 3,
+        input_output_aliases={4: 0},
+        scratch_shapes=near_scratch,
         compiler_params=params,
-        name="targets",
-    )(table, pos_blocks)
+        name="near_core1",
+    )(*near_operands, far_rows[1])
+    table, row, hits, shares = pl.pallas_call(
+        functools.partial(after_kernel, sizes, early),
+        out_shape=near_types,
+        in_specs=near_specs + [smem()] + [vmem()] * 3,
+        out_specs=[smem()] + [vmem()] * 3,
+        scratch_shapes=near_scratch,
+        compiler_params=params,
+        name="near_core0",
+    )(*near_operands, table, row, hits, shares)
+    rows = [row, swap_dp(far_rows[0], 1), swap_dp(sent[0], 2)]
+    rows += [swap_dp(x, (k + 1) & ~1) for k, x in enumerate(handed) if k >= 2]
+
+    feat_blocks = feats.reshape(block_count, BLK, width)
     kept = []
     stats = []
     for slots in groups:

time: 66.8 us -> 70.9 us (1.061)
  starting transfers between devices: 13 us -> 14.7 us
  blocking collectives: 12.4 us -> 13.2 us
  local copies, waits for them, and re-layouts: 0.02 us -> 0.73 us
    ppermute x3 -> x4, waiting for transfers between devices: 16.6 us -> 13.5 us  [swap_dp(): return lax.ppermute(x, 'dp', [(i, i ^ mask) for i in range(dp_count)])]
    ppermute x3 -> x4, starting transfers between devices: 3.24 us -> 5.88 us  [swap_dp(): return lax.ppermute(x, 'dp', [(i, i ^ mask) for i in range(dp_count)])]
    ppermute x2, waiting for transfers between devices: 6.87 us -> 8.86 us  [shards(): got = lax.ppermute(send, 'label', [(i, i ^ 1) for i in range(lab_count)])]
    ppermute x6, waiting for transfers between devices: 2.55 us -> 3.87 us  [shards(): finals.append(lax.ppermute(outgoing[j - 1], 'label', hop))]
    ppermute x6, starting transfers between devices: 8.91 us -> 8.01 us  [shards(): finals.append(lax.ppermute(outgoing[j - 1], 'label', hop))]
    all_to_all x1, blocking collectives: 12.4 us -> 13.2 us  [shards(): lax.all_to_all(stats[0], 'label', split_axis=0, concat_axis=0, tiled=True)]
    unnamed x10 -> x12, local copies, waits for them, and re-layouts: 0.02 us -> 0.73 us
  transfers between devices with their start and end apart: 11 -> 12, of which waited for: 6 -> 7; matrix products, arithmetic and copies ran while one was open for 0% -> 0% of each run, Pallas kernels for 12% -> 12%
where the time goes in v3:
time: 70.9 us; the launch traced here: 70.6 us
  waiting for transfers between devices  26.2 us (37%)
  Pallas kernels  15 us (21%)
  starting transfers between devices  14.7 us (21%)
  blocking collectives  13.2 us (19%)
  local copies, waits for them, and re-layouts  0.73 us (1%)
  between operations  0.72 us (1%)
    ppermute x4, waiting for transfers between devices, swap_dp(): return lax.ppermute(x, 'dp', [(i, i ^ mask) for i in range(dp_count)])  13.5 us
    all_to_all x1, blocking collectives, shards(): lax.all_to_all(stats[0], 'label', split_axis=0, concat_axis=0, tiled=True)  13.2 us
    ppermute x2, waiting for transfers between devices, shards(): got = lax.ppermute(send, 'label', [(i, i ^ 1) for i in range(lab_count)])  8.86 us
    ppermute x6, starting transfers between devices, shards(): finals.append(lax.ppermute(outgoing[j - 1], 'label', hop))  8.01 us
    ppermute x4, starting transfers between devices, swap_dp(): return lax.ppermute(x, 'dp', [(i, i ^ mask) for i in range(dp_count)])  5.88 us
    ppermute x6, waiting for transfers between devices, shards(): finals.append(lax.ppermute(outgoing[j - 1], 'label', hop))  3.87 us
    pallas_call x2, Pallas kernels, shards(): pl.pallas_call(functools.partial(half_kernel, side, groups, lab_count, po...  3.58 us
    pallas_call x3, Pallas kernels, shards(): pl.pallas_call(functools.partial(logit_kernel, slots, not last, copies),...  3.57 us
  transfers between devices with their start and end apart: 12, of which 7 were waited for; matrix products, arithmetic and copies ran while one was open for 0% of the time, Pallas kernels for 12%

profile of v3, /device:TPU:0, one launch (start us, length us, event | category | flops | bytes accessed | tf_op | source)
XLA Modules:
  0.0 70.6 jit_solution(2072677534773294218)
XLA Ops:
  0.6 0.0 copy-start
  0.6 0.0 copy-start.2
  0.7 0.0 copy-start.4
  0.7 3.0 %pick_far.1 = (bf16[256,1024]{1,0:T(8,128)(2,1)}, bf16[256,1024]{1,0:T(8,128)(2,1)}, bf16[256,1024]{1,0:T(8,128)(2,1)}) custom-call(s32[16,16]{1,0:T(8,128)} %lists.3, s32[128]{0:T(128)} %slots.3, bf16[4,256,1024]{2,1,0:T(8,128)(2,1)} %weights.3), custom_call_target="tpu_custom_call" | custom-call | tf_op jit(solution)/shard_map/pick_far/pallas_call | solution.py:351
  3.6 0.5 collective-permute-start
  4.2 0.0 copy-done
  4.2 0.0 copy-done.2
  4.2 0.0 copy-done.4
  4.2 0.0 copy-start.3
  4.2 0.7 %copy-done.3 = s32[512,8]{0,1:T(8,128)S(1)} copy-done((s32[512,8]{0,1:T(8,128)S(1)}, s32[512,8]{0,1:T(8,128)}, u32[]{:S(2)}) %copy-start.3) | copy-done | bytes 16408
  4.9 0.0 copy-start.5
  4.9 0.6 near_core1.1
  5.5 2.6 %collective-permute-start.3 = (bf16[256,1024]{1,0:T(8,128)(2,1)}, bf16[256,1024]{1,0:T(8,128)(2,1)S(1)}, u32[]{:S(2)}, u32[]{:S(2)}) collective-permute-start(bf16[256,1024]{1,0:T(8,128)(2,1)} %get-tuple-element.45), channel_id=1, source_target_pairs={{0,16},{8,24},{16,0},{24,8},{1,17},{9,25},{17,1},{25,9},{2,18},{10... | collective-permute-start | bytes 1572872 | tf_op jit(solution)/shard_map/ppermute | solution.py:386
  8.2 0.0 copy-done.5
  8.2 2.4 %collective-permute-start.2 = (bf16[256,1024]{1,0:T(8,128)(2,1)S(1)}, bf16[256,1024]{1,0:T(8,128)(2,1)S(1)}, u32[]{:S(2)}, u32[]{:S(2)}) collective-permute-start(bf16[256,1024]{1,0:T(8,128)(2,1)S(1)} %copy-done.5), channel_id=1, source_target_pairs={{0,8},{8,0},{16,24},{24,16},{1,9},{9,1},{17,25},{25,17},{2,10},{10... | collective-permute-start | bytes 1572872 | tf_op jit(solution)/shard_map/ppermute | solution.py:386
  10.5 0.0 collective-permute-done
  10.5 0.4 collective-permute-start.1
  10.9 0.0 copy-start.1
  10.9 3.4 %near_core0.1 = (s32[4,4]{1,0:T(4,128)S(1)}, bf16[256,1024]{1,0:T(8,128)(2,1)S(1)}, f32[4,256,256]{2,1,0:T(8,128)S(1)}, f32[3,256,256]{2,1,0:T(8,128)S(1)}) custom-call(s32[16,16]{1,0:T(8,128)S(1)} %copy-done.2, s32[128]{0:T(128)S(1)} %copy-done.4, bf16[4,256,1024]{2,1,0:T(8,128)(2,1)S(1)} %copy-done, s32[4,8,128]{2,1,0:T(8,128)S(1)} %bitcast.9, ...), custom_call_target="tpu_custom_call" | custom-call | tf_op jit(solution)/shard_map/near_core0/pallas_call | solution.py:399
  14.3 4.8 %collective-permute-done.3.rest_0_.rest_5_ = bf16[256,1024]{1,0:T(8,128)(2,1)S(1)} collective-permute-done((bf16[256,1024]{1,0:T(8,128)(2,1)}, bf16[256,1024]{1,0:T(8,128)(2,1)S(1)}, u32[]{:S(2)}, u32[]{:S(2)}) %collective-permute-start.3) | collective-permute-done | bytes 524320 | tf_op jit(solution)/shard_map/ppermute | solution.py:386
  19.1 0.0 copy-done.1
  19.1 1.1 %logits.3 = (f32[1,256,256]{2,1,0:T(8,128)S(1)}, f32[1,3,4,128]{3,2,1,0:T(4,128)S(1)}) custom-call(s32[4,4]{1,0:T(4,128)S(1)} %get-tuple-element.39.table_ref, bf16[4,128,1024]{2,1,0:T(8,128)(2,1)S(1)} %bitcast.5, f32[4,256,256]{2,1,0:T(8,128)S(1)} %get-tuple-element.40.hits_ref, bf16[256,1024]{1,0:T(8,128)(2,1)S(1)} %collective-permute-done.3.rest_0_.rest_5_), custom_call_target="tpu_custom_call" | custom-call | flops 134217728 | bytes 524288 | tf_op jit(solution)/shard_map/logits/pallas_call | solution.py:419
  20.2 0.0 collective-permute-done.2.rest_1_.rest_4_
  20.2 1.4 %logits.4 = (f32[2,256,256]{2,1,0:T(8,128)S(1)}, f32[1,3,4,128]{3,2,1,0:T(4,128)S(1)}) custom-call(s32[4,4]{1,0:T(4,128)S(1)} %get-tuple-element.39.table_ref, bf16[4,128,1024]{2,1,0:T(8,128)(2,1)S(1)} %bitcast.6, f32[4,256,256]{2,1,0:T(8,128)S(1)} %get-tuple-element.40.hits_ref, bf16[256,1024]{1,0:T(8,128)(2,1)S(1)} %get-tuple-element.43.rest_0_.rest_3_, ...), custom_call_target="tpu_custom_call" | custom-call | flops 268435456 | bytes 1048576 | tf_op jit(solution)/shard_map/logits/pallas_call | solution.py:419
  21.6 8.7 %collective-permute-done.1.rest_0_.rest_6_ = bf16[256,1024]{1,0:T(8,128)(2,1)S(1)} collective-permute-done((bf16[256,1024]{1,0:T(8,128)(2,1)S(1)}, bf16[256,1024]{1,0:T(8,128)(2,1)S(1)}, u32[]{:S(2)}, u32[]{:S(2)}) %collective-permute-start.1) | collective-permute-done | bytes 524320 | tf_op jit(solution)/shard_map/ppermute | solution.py:386
  30.3 1.1 %logits.5 = (f32[1,256,256]{2,1,0:T(8,128)S(1)}, f32[8,3,4,128]{3,2,1,0:T(4,128)S(1)}) custom-call(s32[4,4]{1,0:T(4,128)S(1)} %get-tuple-element.39.table_ref, bf16[4,128,1024]{2,1,0:T(8,128)(2,1)S(1)} %bitcast.7, f32[4,256,256]{2,1,0:T(8,128)S(1)} %get-tuple-element.40.hits_ref, bf16[256,1024]{1,0:T(8,128)(2,1)S(1)} %collective-permute-done.1.rest_0_.rest_6_, ...), custom_call_target="tpu_custom_call" | custom-call | flops 134217728 | bytes 524288 | tf_op jit(solution)/shard_map/logits/pallas_call | solution.py:419
  31.4 13.2 %all_to_all.5.stats_ref = f32[8,3,4,128]{3,2,1,0:T(4,128)S(1)} all-to-all(f32[8,3,4,128]{3,2,1,0:T(4,128)S(1)} %get-tuple-element.48), channel_id=1, replica_groups=mesh['dp'=4,'label'=8] {'label'}, dimensions={0} | all-to-all | bytes 98304 | tf_op jit(solution)/shard_map/all_to_all | solution.py:439
  44.6 1.8 %grads.3 = (f32[4,128]{1,0:T(4,128)}, f32[4,256,128]{2,1,0:T(8,128)S(1)}, bf16[4,256,128]{2,1,0:T(8,128)(2,1)S(1)}) custom-call(s32[4,4]{1,0:T(4,128)S(1)} %get-tuple-element.39.table_ref, f32[4,256,256]{2,1,0:T(8,128)S(1)} %get-tuple-element.40.hits_ref, f32[3,256,256]{2,1,0:T(8,128)S(1)} %get-tuple-element.41.shares_ref, ...), custom_call_target="tpu_custom_call" | custom-call | flops 268435456 | bytes 2097152 | tf_op jit(solution)/shard_map/grads/pallas_call | solution.py:470
  46.4 0.4 collective-permute-start.4
  46.8 1.8 %grads.2 = (f32[4,128]{1,0:T(4,128)}, f32[4,256,128]{2,1,0:T(8,128)S(1)}, bf16[4,256,128]{2,1,0:T(8,128)(2,1)S(1)}) custom-call(s32[4,4]{1,0:T(4,128)S(1)} %get-tuple-element.39.table_ref, f32[4,256,256]{2,1,0:T(8,128)S(1)} %get-tuple-element.40.hits_ref, f32[3,256,256]{2,1,0:T(8,128)S(1)} %get-tuple-element.41.shares_ref, ...), custom_call_target="tpu_custom_call" | custom-call | flops 268435456 | bytes 2097152 | tf_op jit(solution)/shard_map/grads/pallas_call | solution.py:470
  48.6 6.2 %collective-permute-done.4.got_ref = bf16[4,256,128]{2,1,0:T(8,128)(2,1)S(1)} collective-permute-done((bf16[4,256,128]{2,1,0:T(8,128)(2,1)S(1)}, bf16[4,256,128]{2,1,0:T(8,128)(2,1)S(1)}, u32[]{:S(2)}, u32[]{:S(2)}) %collective-permute-start.4) | collective-permute-done | bytes 262176 | tf_op jit(solution)/shard_map/ppermute | solution.py:494
  54.8 0.4 collective-permute-start.8
  55.3 0.1 pair_sums.2
  55.3 0.8 %collective-permute-start.5 = (bf16[256,128]{1,0:T(8,128)(2,1)S(1)}, bf16[256,128]{1,0:T(8,128)(2,1)S(1)}, u32[]{:S(2)}, u32[]{:S(2)}) collective-permute-start(bf16[256,128]{1,0:T(8,128)(2,1)S(1)} %get-tuple-element.56), channel_id=1, source_target_pairs={{0,2},{1,3},{2,0},{3,1},{4,6},{5,7},{6,4},{7,5},{8,10},{9,11},{10,... | collective-permute-start | bytes 196616 | tf_op jit(solution)/shard_map/ppermute | solution.py:507
  56.1 1.0 %collective-permute-start.6 = (bf16[256,128]{1,0:T(8,128)(2,1)S(1)}, bf16[256,128]{1,0:T(8,128)(2,1)S(1)}, u32[]{:S(2)}, u32[]{:S(2)}) collective-permute-start(bf16[256,128]{1,0:T(8,128)(2,1)S(1)} %get-tuple-element.57), channel_id=1, source_target_pairs={{0,4},{1,5},{2,6},{3,7},{4,0},{5,1},{6,2},{7,3},{8,12},{9,13},{10,... | collective-permute-start | bytes 196616 | tf_op jit(solution)/shard_map/ppermute | solution.py:507
  57.1 2.6 %collective-permute-start.7 = (bf16[256,128]{1,0:T(8,128)(2,1)S(1)}, bf16[256,128]{1,0:T(8,128)(2,1)S(1)}, u32[]{:S(2)}, u32[]{:S(2)}) collective-permute-start(bf16[256,128]{1,0:T(8,128)(2,1)S(1)} %get-tuple-element.58), channel_id=1, source_target_pairs={{0,6},{1,7},{2,4},{3,5},{4,2},{5,3},{6,0},{7,1},{8,14},{9,15},{10,... | collective-permute-start | bytes 196616 | tf_op jit(solution)/shard_map/ppermute | solution.py:507
  59.8 2.7 %collective-permute-done.8.got_ref = bf16[4,256,128]{2,1,0:T(8,128)(2,1)S(1)} collective-permute-done((bf16[4,256,128]{2,1,0:T(8,128)(2,1)S(1)}, bf16[4,256,128]{2,1,0:T(8,128)(2,1)S(1)}, u32[]{:S(2)}, u32[]{:S(2)}) %collective-permute-start.8) | collective-permute-done | bytes 262176 | tf_op jit(solution)/shard_map/ppermute | solution.py:494
  62.5 0.6 collective-permute-start.10
  63.0 2.2 %collective-permute-start.11 = (bf16[256,128]{1,0:T(8,128)(2,1)S(1)}, bf16[256,128]{1,0:T(8,128)(2,1)S(1)}, u32[]{:S(2)}, u32[]{:S(2)}) collective-permute-start(bf16[256,128]{1,0:T(8,128)(2,1)S(1)} %get-tuple-element.65), channel_id=1, source_target_pairs={{0,6},{1,7},{2,4},{3,5},{4,2},{5,3},{6,0},{7,1},{8,14},{9,15},{10,... | collective-permute-start | bytes 196616 | tf_op jit(solution)/shard_map/ppermute | solution.py:507
  65.2 0.0 collective-permute-done.5.refs_1_
  65.2 0.8 %collective-permute-start.9 = (bf16[256,128]{1,0:T(8,128)(2,1)S(1)}, bf16[256,128]{1,0:T(8,128)(2,1)S(1)}, u32[]{:S(2)}, u32[]{:S(2)}) collective-permute-start(bf16[256,128]{1,0:T(8,128)(2,1)S(1)} %get-tuple-element.63), channel_id=1, source_target_pairs={{0,2},{1,3},{2,0},{3,1},{4,6},{5,7},{6,4},{7,5},{8,10},{9,11},{10,... | collective-permute-start | bytes 196616 | tf_op jit(solution)/shard_map/ppermute | solution.py:507
  66.0 0.0 collective-permute-done.6.refs_2_
  66.0 0.0 collective-permute-done.7.refs_3_
  66.0 2.4 %collective-permute-done.10.refs_6_ = bf16[256,128]{1,0:T(8,128)(2,1)S(1)} collective-permute-done((bf16[256,128]{1,0:T(8,128)(2,1)S(1)}, bf16[256,128]{1,0:T(8,128)(2,1)S(1)}, u32[]{:S(2)}, u32[]{:S(2)}) %collective-permute-start.10) | collective-permute-done | bytes 65568 | tf_op jit(solution)/shard_map/ppermute | solution.py:507
  68.5 0.8 %collective-permute-done.11.refs_7_ = bf16[256,128]{1,0:T(8,128)(2,1)S(1)} collective-permute-done((bf16[256,128]{1,0:T(8,128)(2,1)S(1)}, bf16[256,128]{1,0:T(8,128)(2,1)S(1)}, u32[]{:S(2)}, u32[]{:S(2)}) %collective-permute-start.11) | collective-permute-done | bytes 65568 | tf_op jit(solution)/shard_map/ppermute | solution.py:507
  69.2 0.7 collective-permute-done.9.refs_5_
  69.9 0.7 %last_sums.1 = bf16[512,128]{1,0:T(8,128)(2,1)} custom-call(f32[256,128]{1,0:T(8,128)S(1)} %get-tuple-element.55.refs_0_, bf16[256,128]{1,0:T(8,128)(2,1)S(1)} %collective-permute-done.5.refs_1_, bf16[256,128]{1,0:T(8,128)(2,1)S(1)} %collective-permute-done.6.refs_2_, bf16[256,128]{1,0:T(8,128)(2,1)S(1)} %collective-permute-done.7.refs_3_, ...), custom_call_target="tpu_custom_call" | custom-call | tf_op jit(solution)/shard_map/last_sums/pallas_call | solution.py:508
  (1 shorter events, 0.0 us)
Async XLA Ops:
  0.6 3.5 %copy-start = (bf16[4,256,1024]{2,1,0:T(8,128)(2,1)S(1)}, bf16[4,256,1024]{2,1,0:T(8,128)(2,1)}, u32[]{:S(2)}) copy-start(bf16[4,256,1024]{2,1,0:T(8,128)(2,1)} %weights.3) | copy-start | bytes 6291460
  0.6 3.5 %copy-start.2 = (s32[16,16]{1,0:T(8,128)S(1)}, s32[16,16]{1,0:T(8,128)}, u32[]{:S(2)}) copy-start(s32[16,16]{1,0:T(8,128)} %lists.3) | copy-start | bytes 3076
  0.7 3.5 %copy-start.4 = (s32[128]{0:T(128)S(1)}, s32[128]{0:T(128)}, u32[]{:S(2)}) copy-start(s32[128]{0:T(128)} %slots.3) | copy-start | bytes 1540
  3.6 6.9 %collective-permute-start = (bf16[256,1024]{1,0:T(8,128)(2,1)}, bf16[256,1024]{1,0:T(8,128)(2,1)S(1)}, u32[]{:S(2)}, u32[]{:S(2)}) collective-permute-start(bf16[256,1024]{1,0:T(8,128)(2,1)} %get-tuple-element.42), channel_id=1, source_target_pairs={{0,8},{8,0},{16,24},{24,16},{1,9},{9,1},{17,25},{25,17},{2,10},{10... | collective-permute-start | bytes 1572872 | tf_op jit(solution)/shard_map/ppermute | solution.py:386
  4.2 0.7 %copy-start.3 = (s32[512,8]{0,1:T(8,128)S(1)}, s32[512,8]{0,1:T(8,128)}, u32[]{:S(2)}) copy-start(s32[512,8]{0,1:T(8,128)} %param.9) | copy-start | bytes 49156
  4.9 3.3 %copy-start.5 = (bf16[256,1024]{1,0:T(8,128)(2,1)S(1)}, bf16[256,1024]{1,0:T(8,128)(2,1)}, u32[]{:S(2)}) copy-start(bf16[256,1024]{1,0:T(8,128)(2,1)} %get-tuple-element.44) | copy-start | bytes 1572868
  5.5 13.6 %collective-permute-start.3 = (bf16[256,1024]{1,0:T(8,128)(2,1)}, bf16[256,1024]{1,0:T(8,128)(2,1)S(1)}, u32[]{:S(2)}, u32[]{:S(2)}) collective-permute-start(bf16[256,1024]{1,0:T(8,128)(2,1)} %get-tuple-element.45), channel_id=1, source_target_pairs={{0,16},{8,24},{16,0},{24,8},{1,17},{9,25},{17,1},{25,9},{2,18},{10... | collective-permute-start | bytes 1572872 | tf_op jit(solution)/shard_map/ppermute | solution.py:386
  8.2 12.1 %collective-permute-start.2 = (bf16[256,1024]{1,0:T(8,128)(2,1)S(1)}, bf16[256,1024]{1,0:T(8,128)(2,1)S(1)}, u32[]{:S(2)}, u32[]{:S(2)}) collective-permute-start(bf16[256,1024]{1,0:T(8,128)(2,1)S(1)} %copy-done.5), channel_id=1, source_target_pairs={{0,8},{8,0},{16,24},{24,16},{1,9},{9,1},{17,25},{25,17},{2,10},{10... | collective-permute-start | bytes 1572872 | tf_op jit(solution)/shard_map/ppermute | solution.py:386
  10.5 19.8 %collective-permute-start.1 = (bf16[256,1024]{1,0:T(8,128)(2,1)S(1)}, bf16[256,1024]{1,0:T(8,128)(2,1)S(1)}, u32[]{:S(2)}, u32[]{:S(2)}) collective-permute-start(bf16[256,1024]{1,0:T(8,128)(2,1)S(1)} %collective-permute-done), channel_id=1, source_target_pairs={{0,16},{8,24},{16,0},{24,8},{1,17},{9,25},{17,1},{25,9},{2,18},{10... | collective-permute-start | bytes 1572872 | tf_op jit(solution)/shard_map/ppermute | solution.py:386
  10.9 8.2 %copy-start.1 = (bf16[512,1024]{1,0:T(8,128)(2,1)S(1)}, bf16[512,1024]{1,0:T(8,128)(2,1)}, u32[]{:S(2)}) copy-start(bf16[512,1024]{1,0:T(8,128)(2,1)} %param.5) | copy-start | bytes 3145732
  46.4 8.4 %collective-permute-start.4 = (bf16[4,256,128]{2,1,0:T(8,128)(2,1)S(1)}, bf16[4,256,128]{2,1,0:T(8,128)(2,1)S(1)}, u32[]{:S(2)}, u32[]{:S(2)}) collective-permute-start(bf16[4,256,128]{2,1,0:T(8,128)(2,1)S(1)} %get-tuple-element.54), channel_id=1, source_target_pairs={{0,1},{1,0},{2,3},{3,2},{4,5},{5,4},{6,7},{7,6},{8,9},{9,8},{10,11... | collective-permute-start | bytes 786440 | tf_op jit(solution)/shard_map/ppermute | solution.py:494
  54.8 7.6 %collective-permute-start.8 = (bf16[4,256,128]{2,1,0:T(8,128)(2,1)S(1)}, bf16[4,256,128]{2,1,0:T(8,128)(2,1)S(1)}, u32[]{:S(2)}, u32[]{:S(2)}) collective-permute-start(bf16[4,256,128]{2,1,0:T(8,128)(2,1)S(1)} %get-tuple-element.61), channel_id=1, source_target_pairs={{0,1},{1,0},{2,3},{3,2},{4,5},{5,4},{6,7},{7,6},{8,9},{9,8},{10,11... | collective-permute-start | bytes 786440 | tf_op jit(solution)/shard_map/ppermute | solution.py:494
  55.3 9.9 %collective-permute-start.5 = (bf16[256,128]{1,0:T(8,128)(2,1)S(1)}, bf16[256,128]{1,0:T(8,128)(2,1)S(1)}, u32[]{:S(2)}, u32[]{:S(2)}) collective-permute-start(bf16[256,128]{1,0:T(8,128)(2,1)S(1)} %get-tuple-element.56), channel_id=1, source_target_pairs={{0,2},{1,3},{2,0},{3,1},{4,6},{5,7},{6,4},{7,5},{8,10},{9,11},{10,... | collective-permute-start | bytes 196616 | tf_op jit(solution)/shard_map/ppermute | solution.py:507
  56.1 9.9 %collective-permute-start.6 = (bf16[256,128]{1,0:T(8,128)(2,1)S(1)}, bf16[256,128]{1,0:T(8,128)(2,1)S(1)}, u32[]{:S(2)}, u32[]{:S(2)}) collective-permute-start(bf16[256,128]{1,0:T(8,128)(2,1)S(1)} %get-tuple-element.57), channel_id=1, source_target_pairs={{0,4},{1,5},{2,6},{3,7},{4,0},{5,1},{6,2},{7,3},{8,12},{9,13},{10,... | collective-permute-start | bytes 196616 | tf_op jit(solution)/shard_map/ppermute | solution.py:507
  57.1 8.9 %collective-permute-start.7 = (bf16[256,128]{1,0:T(8,128)(2,1)S(1)}, bf16[256,128]{1,0:T(8,128)(2,1)S(1)}, u32[]{:S(2)}, u32[]{:S(2)}) collective-permute-start(bf16[256,128]{1,0:T(8,128)(2,1)S(1)} %get-tuple-element.58), channel_id=1, source_target_pairs={{0,6},{1,7},{2,4},{3,5},{4,2},{5,3},{6,0},{7,1},{8,14},{9,15},{10,... | collective-permute-start | bytes 196616 | tf_op jit(solution)/shard_map/ppermute | solution.py:507
  62.5 6.0 %collective-permute-start.10 = (bf16[256,128]{1,0:T(8,128)(2,1)S(1)}, bf16[256,128]{1,0:T(8,128)(2,1)S(1)}, u32[]{:S(2)}, u32[]{:S(2)}) collective-permute-start(bf16[256,128]{1,0:T(8,128)(2,1)S(1)} %get-tuple-element.64), channel_id=1, source_target_pairs={{0,4},{1,5},{2,6},{3,7},{4,0},{5,1},{6,2},{7,3},{8,12},{9,13},{10,... | collective-permute-start | bytes 196616 | tf_op jit(solution)/shard_map/ppermute | solution.py:507
  63.0 6.2 %collective-permute-start.11 = (bf16[256,128]{1,0:T(8,128)(2,1)S(1)}, bf16[256,128]{1,0:T(8,128)(2,1)S(1)}, u32[]{:S(2)}, u32[]{:S(2)}) collective-permute-start(bf16[256,128]{1,0:T(8,128)(2,1)S(1)} %get-tuple-element.65), channel_id=1, source_target_pairs={{0,6},{1,7},{2,4},{3,5},{4,2},{5,3},{6,0},{7,1},{8,14},{9,15},{10,... | collective-permute-start | bytes 196616 | tf_op jit(solution)/shard_map/ppermute | solution.py:507
  65.2 4.7 %collective-permute-start.9 = (bf16[256,128]{1,0:T(8,128)(2,1)S(1)}, bf16[256,128]{1,0:T(8,128)(2,1)S(1)}, u32[]{:S(2)}, u32[]{:S(2)}) collective-permute-start(bf16[256,128]{1,0:T(8,128)(2,1)S(1)} %get-tuple-element.63), channel_id=1, source_target_pairs={{0,2},{1,3},{2,0},{3,1},{4,6},{5,7},{6,4},{7,5},{8,10},{9,11},{10,... | collective-permute-start | bytes 196616 | tf_op jit(solution)/shard_map/ppermute | solution.py:507

commit v4 on v1

--- a/solution.py
+++ b/solution.py
@@ -103,7 +103,7 @@
         copy.wait()
 
 
-def target_kernel(early, table_ref, pos_ref, hits_ref, shares_ref):
+def target_kernel(early, late, table_ref, pos_ref, feats_ref, hits_ref, shares_ref, turned_ref):
     count, cluster_size, _ = hits_ref.shape
     pos_count = pos_ref.shape[1]
 
@@ -119,6 +119,9 @@
             hits_ref[s, :, columns] = hits
             if s in early:
                 shares_ref[early.index(s), columns, :] = (hits / pos_count).T
+            else:
+                feats = feats_ref[table_ref[s, 1 + side]].astype(jnp.float32)
+                turned_ref[late.index(s), :, columns] = feats.T.astype(jnp.bfloat16)
 
     for s in range(count):
         pl.when(table_ref[s, 0] >= 0)(functools.partial(one_slot, s))
@@ -135,19 +138,21 @@
     else:
         stats_ref[...] = rest[count][0]
     for i, (s, ref) in enumerate(zip(slots, rows)):
+        if not turned:
+            logits_ref[i] = jnp.dot(ref[...], feats_ref[i], preferred_element_type=jnp.float32)
         for side in range(2):
             block = table_ref[s, 1 + side]
-            logits = lax.dot_general(
-                ref[...],
-                feats_ref[block],
-                (((1,), (1,)), ((), ())),
-                preferred_element_type=jnp.float32,
-            )
             columns = pl.ds(side * BLK, BLK)
             if turned:
+                logits = lax.dot_general(
+                    ref[...],
+                    feats_ref[block],
+                    (((1,), (1,)), ((), ())),
+                    preferred_element_type=jnp.float32,
+                )
                 logits_ref[i, columns, :] = logits.T
             else:
-                logits_ref[i, :, columns] = logits
+                logits = logits_ref[i, :, columns]
             highest = jnp.max(logits, axis=0, keepdims=True)
             total = jnp.sum(jnp.exp(logits - highest), axis=0, keepdims=True)
             positive = jnp.sum(hits_ref[s, :, columns] * logits, axis=0, keepdims=True)
@@ -175,13 +180,12 @@
     return highest + jnp.log(summed), positive
 
 
-def prepare(stats_ref, pos_count, lab_count, loss_ref, lse_ref, columns_ref, total_ref, first):
+def prepare(stats_ref, pos_count, lab_count, loss_ref, lse_ref, columns_ref, first):
     lse, positive = row_sums(stats_ref, lab_count)
     lse_ref[...] = lse
     loss_ref[...] = lse - positive / pos_count
     for b in range(columns_ref.shape[0]):
         columns_ref[b] = jnp.broadcast_to(lse[first + b : first + b + 1, :], (BLK, BLK)).T
-    total_ref[...] = jnp.zeros_like(total_ref)
 
 
 def add_slots(sides, groups, pos_count, first, table_ref, hits_ref, shares_ref, logits_refs, rows, sums):
@@ -217,25 +221,50 @@
                 pl.when(table_ref[s, 0] >= 0)(body)
 
 
+def half_sums(side, groups, pos_count, table_ref, hits_ref, shares_ref, logits_refs, rows, sums):
+    lse_ref, columns_ref, dlogit_ref, total_ref = sums
+    half = columns_ref.shape[0]
+    cluster_size = rows[0].shape[0]
+    early = [s for slots in groups[:-1] for s in slots]
+    here = pl.ds(side * BLK, BLK)
+    dlogit_ref[...] = jnp.zeros_like(dlogit_ref)
+    for slots, logits_ref in zip(groups, logits_refs):
+        for i, s in enumerate(slots):
+            block = table_ref[s, 1 + side]
+            if s in early:
+                column = columns_ref[block - side * half]
+                column = jnp.concatenate([column] * (cluster_size // BLK), axis=1)
+                dlogit = jnp.exp(logits_ref[i, here, :] - column) - shares_ref[early.index(s), here, :]
+            else:
+                row = lse_ref[pl.ds(block, 1), :]
+                dlogit = jnp.exp(logits_ref[i, :, here] - row) - hits_ref[s, :, here] / pos_count
+                dlogit = dlogit.T
+            at = pl.ds(pl.multiple_of((block - side * half) * BLK, BLK), BLK)
+            labels = pl.ds(s * cluster_size, cluster_size)
+            dlogit_ref[at, labels] = dlogit.astype(jnp.bfloat16)
+    total_ref[...] = jnp.dot(
+        dlogit_ref[...],
+        jnp.concatenate([ref[...] for ref in rows], axis=0),
+        preferred_element_type=jnp.float32,
+    )
+
+
 def half_kernel(side, groups, lab_count, pos_count, table_ref, hits_ref, shares_ref, stats_ref, *rest):
     logits_refs = rest[: len(groups)]
-    rows = rest[len(groups) : -6]
-    loss_ref, keep_ref, send_ref, lse_ref, columns_ref, total_ref = rest[-6:]
-    half = total_ref.shape[0]
-    prepare(
-        stats_ref, pos_count, lab_count, loss_ref, lse_ref, columns_ref, total_ref, side * half
-    )
-    add_slots(
-        (side,),
+    rows = rest[len(groups) : -7]
+    loss_ref, keep_ref, send_ref, lse_ref, columns_ref, dlogit_ref, total_ref = rest[-7:]
+    half = columns_ref.shape[0]
+    prepare(stats_ref, pos_count, lab_count, loss_ref, lse_ref, columns_ref, side * half)
+    half_sums(
+        side,
         groups,
         pos_count,
-        side * half,
         table_ref,
         hits_ref,
         shares_ref,
         logits_refs,
         rows,
-        (lse_ref, columns_ref, total_ref),
+        (lse_ref, columns_ref, dlogit_ref, total_ref),
     )
     part = keep_ref.shape[2]
     lab_index = lax.axis_index("label")
@@ -244,8 +273,8 @@
         other = pl.ds(pl.multiple_of((lab_index ^ (2 * j + 1)) * part, part), part)
         for b in range(half):
             here = pl.ds(b * BLK, BLK)
-            keep_ref[j, here, :] = total_ref[b, :, mine]
-            send_ref[j, here, :] = total_ref[b, :, other].astype(jnp.bfloat16)
+            keep_ref[j, here, :] = total_ref[here, mine]
+            send_ref[j, here, :] = total_ref[here, other].astype(jnp.bfloat16)
 
 
 def pair_kernel(keep_ref, got_ref, *outs):
@@ -268,7 +297,8 @@
     logits_refs = rest[: len(groups)]
     rows = rest[len(groups) : -5]
     loss_ref, out_ref, lse_ref, columns_ref, total_ref = rest[-5:]
-    prepare(stats_ref, pos_count, lab_count, loss_ref, lse_ref, columns_ref, total_ref, 0)
+    prepare(stats_ref, pos_count, lab_count, loss_ref, lse_ref, columns_ref, 0)
+    total_ref[...] = jnp.zeros_like(total_ref)
     add_slots(
         (0, 1),
         groups,
@@ -349,17 +379,19 @@
     if dp_count == 4:
         groups = [(2,), (0, 1), (3,)]
     early = [s for slots in groups[:-1] for s in slots]
-    hits, shares = pl.pallas_call(
-        functools.partial(target_kernel, early),
+    late = list(groups[-1])
+    hits, shares, turned = pl.pallas_call(
+        functools.partial(target_kernel, early, late),
         out_shape=[
             jax.ShapeDtypeStruct((dp_count, cluster_size, 2 * BLK), jnp.float32),
             jax.ShapeDtypeStruct((len(early), 2 * BLK, cluster_size), jnp.float32),
+            jax.ShapeDtypeStruct((len(late), width, 2 * BLK), feats.dtype),
         ],
-        in_specs=[smem(), vmem()],
-        out_specs=[vmem()] * 2,
+        in_specs=[smem()] + [vmem()] * 2,
+        out_specs=[vmem()] * 3,
         compiler_params=params,
         name="targets",
-    )(table, pos_blocks)
+    )(table, pos_blocks, feat_blocks)
     kept = []
     stats = []
     for slots in groups:
@@ -383,7 +415,7 @@
                 transcendentals=0,
             ),
             name="logits",
-        )(table, feat_blocks, hits, *[rows[s] for s in slots], *stats)
+        )(table, turned if last else feat_blocks, hits, *[rows[s] for s in slots], *stats)
         kept.append(logits)
         stats = [stats_out]
 
@@ -430,7 +462,8 @@
             scratch_shapes=[
                 lse_scratch,
                 pltpu.VMEM((block_count // 2, BLK, BLK), jnp.float32),
-                pltpu.VMEM((block_count // 2, BLK, width), jnp.float32),
+                pltpu.VMEM((half_rows, dp_count * cluster_size), jnp.bfloat16),
+                pltpu.VMEM((half_rows, width), jnp.float32),
             ],
             compiler_params=params,
             cost_estimate=pl.CostEstimate(

time: 66.8 us -> 66.9 us (level)
  no operation moved by 1% of the time
where the time goes in v4:
time: 66.9 us; the launch traced here: 66.7 us
  waiting for transfers between devices  25.6 us (38%)
  Pallas kernels  14.9 us (22%)
  starting transfers between devices  13 us (19%)
  blocking collectives  12.4 us (19%)
  between operations  0.74 us (1%)
    ppermute x3, waiting for transfers between devices, shards(): rows[k] = lax.ppermute(rows[k], 'dp', [(i, i ^ k) for i in range(dp_count)])  16.4 us
    all_to_all x1, blocking collectives, shards(): lax.all_to_all(stats[0], 'label', split_axis=0, concat_axis=0, tiled=True)  12.4 us
    ppermute x6, starting transfers between devices, shards(): finals.append(lax.ppermute(outgoing[j - 1], 'label', hop))  8.91 us
    ppermute x2, waiting for transfers between devices, shards(): got = lax.ppermute(send, 'label', [(i, i ^ 1) for i in range(lab_count)])  6.6 us
    pallas_call x2, Pallas kernels, shards(): pl.pallas_call(functools.partial(half_kernel, side, groups, lab_count, po...  4.09 us
    pallas_call x3, Pallas kernels, shards(): pl.pallas_call(functools.partial(logit_kernel, slots, not last, copies),...  3.44 us
    ppermute x3, starting transfers between devices, shards(): rows[k] = lax.ppermute(rows[k], 'dp', [(i, i ^ k) for i in range(dp_count)])  3.24 us
    pallas_call x1, Pallas kernels, shards(): pl.pallas_call(functools.partial(far_kernel, sizes, far), out_shape=[row_...  2.97 us
  transfers between devices with their start and end apart: 11, of which 6 were waited for; matrix products, arithmetic and copies ran while one was open for 0% of the time, Pallas kernels for 12%

profile of v4, /device:TPU:0, one launch (start us, length us, event | category | flops | bytes accessed | tf_op | source)
XLA Modules:
  0.0 66.7 jit_solution(6386718152508251845)
XLA Ops:
  0.6 0.0 copy-start.1
  0.6 0.0 copy-start.2
  0.7 0.0 copy-start.4
  0.7 0.0 copy-start
  0.7 0.0 copy-start.3
  0.7 3.0 %pick_far.1 = (bf16[256,1024]{1,0:T(8,128)(2,1)}, bf16[256,1024]{1,0:T(8,128)(2,1)}, bf16[256,1024]{1,0:T(8,128)(2,1)}) custom-call(s32[16,16]{1,0:T(8,128)} %lists_hbm.1, s32[128]{0:T(128)} %slot_hbm.1, bf16[4,256,1024]{2,1,0:T(8,128)(2,1)} %weights_ref.3), custom_call_target="tpu_custom_call" | custom-call | tf_op jit(solution)/shard_map/pick_far/pallas_call | solution.py:348
  3.7 3.0 %collective-permute-start.2 = (bf16[256,1024]{1,0:T(8,128)(2,1)}, bf16[256,1024]{1,0:T(8,128)(2,1)S(1)}, u32[]{:S(2)}, u32[]{:S(2)}) collective-permute-start(bf16[256,1024]{1,0:T(8,128)(2,1)} %get-tuple-element.37), channel_id=1, source_target_pairs={{0,16},{8,24},{16,0},{24,8},{1,17},{9,25},{17,1},{25,9},{2,18},{10... | collective-permute-start | bytes 1572872 | tf_op jit(solution)/shard_map/ppermute | solution.py:373
  6.7 0.0 collective-permute-start.1
  6.7 0.2 collective-permute-start
  6.9 0.0 copy-done.1
  6.9 0.0 copy-done.2
  6.9 0.0 copy-done.4
  6.9 1.6 %pick_near.1 = (s32[4,4]{1,0:T(4,128)S(1)}, bf16[256,1024]{1,0:T(8,128)(2,1)S(1)}) custom-call(s32[16,16]{1,0:T(8,128)S(1)} %copy-done.2, s32[128]{0:T(128)S(1)} %copy-done.4, bf16[4,256,1024]{2,1,0:T(8,128)(2,1)S(1)} %copy-done.1), custom_call_target="tpu_custom_call" | custom-call | tf_op jit(solution)/shard_map/pick_near/pallas_call | solution.py:362
  8.6 0.0 copy-done
  8.6 0.0 copy-done.3
  8.6 1.9 %targets.1 = (f32[4,256,256]{2,1,0:T(8,128)S(1)}, f32[3,256,256]{2,1,0:T(8,128)S(1)}, bf16[1,1024,256]{2,1,0:T(8,128)(2,1)S(1)}) custom-call(s32[4,4]{1,0:T(4,128)S(1)} %get-tuple-element.30.table_ref, s32[4,8,128]{2,1,0:T(8,128)S(1)} %bitcast.8, bf16[4,128,1024]{2,1,0:T(8,128)(2,1)S(1)} %bitcast.5), custom_call_target="tpu_custom_call" | custom-call | tf_op jit(solution)/shard_map/targets/pallas_call | solution.py:383
  10.5 9.1 %collective-permute-done.2.rest_0_.rest_5_ = bf16[256,1024]{1,0:T(8,128)(2,1)S(1)} collective-permute-done((bf16[256,1024]{1,0:T(8,128)(2,1)}, bf16[256,1024]{1,0:T(8,128)(2,1)S(1)}, u32[]{:S(2)}, u32[]{:S(2)}) %collective-permute-start.2) | collective-permute-done | bytes 524320 | tf_op jit(solution)/shard_map/ppermute | solution.py:373
  19.6 1.1 %logits.3 = (f32[1,256,256]{2,1,0:T(8,128)S(1)}, f32[1,3,4,128]{3,2,1,0:T(4,128)S(1)}) custom-call(s32[4,4]{1,0:T(4,128)S(1)} %get-tuple-element.30.table_ref, bf16[4,128,1024]{2,1,0:T(8,128)(2,1)S(1)} %bitcast.6, f32[4,256,256]{2,1,0:T(8,128)S(1)} %get-tuple-element.31.hits_ref, bf16[256,1024]{1,0:T(8,128)(2,1)S(1)} %collective-permute-done.2.rest_0_.rest_5_), custom_call_target="tpu_custom_call" | custom-call | flops 134217728 | bytes 524288 | tf_op jit(solution)/shard_map/logits/pallas_call | solution.py:402
  20.8 0.0 collective-permute-done.1.rest_1_.rest_4_
  20.8 1.4 %logits.4 = (f32[2,256,256]{2,1,0:T(8,128)S(1)}, f32[1,3,4,128]{3,2,1,0:T(4,128)S(1)}) custom-call(s32[4,4]{1,0:T(4,128)S(1)} %get-tuple-element.30.table_ref, bf16[4,128,1024]{2,1,0:T(8,128)(2,1)S(1)} %bitcast.7, f32[4,256,256]{2,1,0:T(8,128)S(1)} %get-tuple-element.31.hits_ref, bf16[256,1024]{1,0:T(8,128)(2,1)S(1)} %get-tuple-element.35.rest_0_.rest_3_, ...), custom_call_target="tpu_custom_call" | custom-call | flops 268435456 | bytes 1048576 | tf_op jit(solution)/shard_map/logits/pallas_call | solution.py:402
  22.1 7.3 %collective-permute-done.rest_0_.rest_6_ = bf16[256,1024]{1,0:T(8,128)(2,1)S(1)} collective-permute-done((bf16[256,1024]{1,0:T(8,128)(2,1)}, bf16[256,1024]{1,0:T(8,128)(2,1)S(1)}, u32[]{:S(2)}, u32[]{:S(2)}) %collective-permute-start) | collective-permute-done | bytes 524320 | tf_op jit(solution)/shard_map/ppermute | solution.py:373
  29.4 0.9 %logits.5 = (f32[1,256,256]{2,1,0:T(8,128)S(1)}, f32[8,3,4,128]{3,2,1,0:T(4,128)S(1)}) custom-call(s32[4,4]{1,0:T(4,128)S(1)} %get-tuple-element.30.table_ref, bf16[1,1024,256]{2,1,0:T(8,128)(2,1)S(1)} %get-tuple-element.33.feats_ref, f32[4,256,256]{2,1,0:T(8,128)S(1)} %get-tuple-element.31.hits_ref, ...), custom_call_target="tpu_custom_call" | custom-call | flops 134217728 | bytes 524288 | tf_op jit(solution)/shard_map/logits/pallas_call | solution.py:402
  30.4 12.4 %all_to_all.5.stats_ref = f32[8,3,4,128]{3,2,1,0:T(4,128)S(1)} all-to-all(f32[8,3,4,128]{3,2,1,0:T(4,128)S(1)} %get-tuple-element.40), channel_id=1, replica_groups=mesh['dp'=4,'label'=8] {'label'}, dimensions={0} | all-to-all | bytes 98304 | tf_op jit(solution)/shard_map/all_to_all | solution.py:422
  42.8 2.0 %grads.3 = (f32[4,128]{1,0:T(4,128)}, f32[4,256,128]{2,1,0:T(8,128)S(1)}, bf16[4,256,128]{2,1,0:T(8,128)(2,1)S(1)}) custom-call(s32[4,4]{1,0:T(4,128)S(1)} %get-tuple-element.30.table_ref, f32[4,256,256]{2,1,0:T(8,128)S(1)} %get-tuple-element.31.hits_ref, f32[3,256,256]{2,1,0:T(8,128)S(1)} %get-tuple-element.32.shares_ref, ...), custom_call_target="tpu_custom_call" | custom-call | flops 268435456 | bytes 2097152 | tf_op jit(solution)/shard_map/grads/pallas_call | solution.py:453
  44.8 0.4 collective-permute-start.3
  45.2 2.0 %grads.2 = (f32[4,128]{1,0:T(4,128)}, f32[4,256,128]{2,1,0:T(8,128)S(1)}, bf16[4,256,128]{2,1,0:T(8,128)(2,1)S(1)}) custom-call(s32[4,4]{1,0:T(4,128)S(1)} %get-tuple-element.30.table_ref, f32[4,256,256]{2,1,0:T(8,128)S(1)} %get-tuple-element.31.hits_ref, f32[3,256,256]{2,1,0:T(8,128)S(1)} %get-tuple-element.32.shares_ref, ...), custom_call_target="tpu_custom_call" | custom-call | flops 268435456 | bytes 2097152 | tf_op jit(solution)/shard_map/grads/pallas_call | solution.py:453
  47.3 5.0 %collective-permute-done.3.got_ref = bf16[4,256,128]{2,1,0:T(8,128)(2,1)S(1)} collective-permute-done((bf16[4,256,128]{2,1,0:T(8,128)(2,1)S(1)}, bf16[4,256,128]{2,1,0:T(8,128)(2,1)S(1)}, u32[]{:S(2)}, u32[]{:S(2)}) %collective-permute-start.3) | collective-permute-done | bytes 262176 | tf_op jit(solution)/shard_map/ppermute | solution.py:478
  52.3 0.4 collective-permute-start.7
  52.7 0.1 pair_sums.2
  52.8 0.8 %collective-permute-start.4 = (bf16[256,128]{1,0:T(8,128)(2,1)S(1)}, bf16[256,128]{1,0:T(8,128)(2,1)S(1)}, u32[]{:S(2)}, u32[]{:S(2)}) collective-permute-start(bf16[256,128]{1,0:T(8,128)(2,1)S(1)} %get-tuple-element.48), channel_id=1, source_target_pairs={{0,2},{1,3},{2,0},{3,1},{4,6},{5,7},{6,4},{7,5},{8,10},{9,11},{10,... | collective-permute-start | bytes 196616 | tf_op jit(solution)/shard_map/ppermute | solution.py:491
  53.6 1.0 %collective-permute-start.5 = (bf16[256,128]{1,0:T(8,128)(2,1)S(1)}, bf16[256,128]{1,0:T(8,128)(2,1)S(1)}, u32[]{:S(2)}, u32[]{:S(2)}) collective-permute-start(bf16[256,128]{1,0:T(8,128)(2,1)S(1)} %get-tuple-element.49), channel_id=1, source_target_pairs={{0,4},{1,5},{2,6},{3,7},{4,0},{5,1},{6,2},{7,3},{8,12},{9,13},{10,... | collective-permute-start | bytes 196616 | tf_op jit(solution)/shard_map/ppermute | solution.py:491
  54.6 2.7 %collective-permute-start.6 = (bf16[256,128]{1,0:T(8,128)(2,1)S(1)}, bf16[256,128]{1,0:T(8,128)(2,1)S(1)}, u32[]{:S(2)}, u32[]{:S(2)}) collective-permute-start(bf16[256,128]{1,0:T(8,128)(2,1)S(1)} %get-tuple-element.50), channel_id=1, source_target_pairs={{0,6},{1,7},{2,4},{3,5},{4,2},{5,3},{6,0},{7,1},{8,14},{9,15},{10,... | collective-permute-start | bytes 196616 | tf_op jit(solution)/shard_map/ppermute | solution.py:491
  57.3 1.6 %collective-permute-done.7.got_ref = bf16[4,256,128]{2,1,0:T(8,128)(2,1)S(1)} collective-permute-done((bf16[4,256,128]{2,1,0:T(8,128)(2,1)S(1)}, bf16[4,256,128]{2,1,0:T(8,128)(2,1)S(1)}, u32[]{:S(2)}, u32[]{:S(2)}) %collective-permute-start.7) | collective-permute-done | bytes 262176 | tf_op jit(solution)/shard_map/ppermute | solution.py:478
  58.9 0.1 pair_sums.3
  58.9 0.9 %collective-permute-start.10 = (bf16[256,128]{1,0:T(8,128)(2,1)S(1)}, bf16[256,128]{1,0:T(8,128)(2,1)S(1)}, u32[]{:S(2)}, u32[]{:S(2)}) collective-permute-start(bf16[256,128]{1,0:T(8,128)(2,1)S(1)} %get-tuple-element.57), channel_id=1, source_target_pairs={{0,6},{1,7},{2,4},{3,5},{4,2},{5,3},{6,0},{7,1},{8,14},{9,15},{10,... | collective-permute-start | bytes 196616 | tf_op jit(solution)/shard_map/ppermute | solution.py:491
  59.8 0.5 collective-permute-start.8
  60.3 0.0 collective-permute-done.4.refs_1_
  60.3 3.1 %collective-permute-start.9 = (bf16[256,128]{1,0:T(8,128)(2,1)S(1)}, bf16[256,128]{1,0:T(8,128)(2,1)S(1)}, u32[]{:S(2)}, u32[]{:S(2)}) collective-permute-start(bf16[256,128]{1,0:T(8,128)(2,1)S(1)} %get-tuple-element.56), channel_id=1, source_target_pairs={{0,4},{1,5},{2,6},{3,7},{4,0},{5,1},{6,2},{7,3},{8,12},{9,13},{10,... | collective-permute-start | bytes 196616 | tf_op jit(solution)/shard_map/ppermute | solution.py:491
  63.4 0.0 collective-permute-done.5.refs_2_
  63.4 0.0 collective-permute-done.6.refs_3_
  63.4 1.8 %collective-permute-done.10.refs_7_ = bf16[256,128]{1,0:T(8,128)(2,1)S(1)} collective-permute-done((bf16[256,128]{1,0:T(8,128)(2,1)S(1)}, bf16[256,128]{1,0:T(8,128)(2,1)S(1)}, u32[]{:S(2)}, u32[]{:S(2)}) %collective-permute-start.10) | collective-permute-done | bytes 65568 | tf_op jit(solution)/shard_map/ppermute | solution.py:491
  65.2 0.8 %collective-permute-done.8.refs_5_ = bf16[256,128]{1,0:T(8,128)(2,1)S(1)} collective-permute-done((bf16[256,128]{1,0:T(8,128)(2,1)S(1)}, bf16[256,128]{1,0:T(8,128)(2,1)S(1)}, u32[]{:S(2)}, u32[]{:S(2)}) %collective-permute-start.8) | collective-permute-done | bytes 65568 | tf_op jit(solution)/shard_map/ppermute | solution.py:491
  66.0 0.0 collective-permute-done.9.refs_6_
  66.0 0.7 %last_sums.1 = bf16[512,128]{1,0:T(8,128)(2,1)} custom-call(f32[256,128]{1,0:T(8,128)S(1)} %get-tuple-element.47.refs_0_, bf16[256,128]{1,0:T(8,128)(2,1)S(1)} %collective-permute-done.4.refs_1_, bf16[256,128]{1,0:T(8,128)(2,1)S(1)} %collective-permute-done.5.refs_2_, bf16[256,128]{1,0:T(8,128)(2,1)S(1)} %collective-permute-done.6.refs_3_, ...), custom_call_target="tpu_custom_call" | custom-call | tf_op jit(solution)/shard_map/last_sums/pallas_call | solution.py:492
Async XLA Ops:
  0.6 6.3 %copy-start.1 = (bf16[4,256,1024]{2,1,0:T(8,128)(2,1)S(1)}, bf16[4,256,1024]{2,1,0:T(8,128)(2,1)}, u32[]{:S(2)}) copy-start(bf16[4,256,1024]{2,1,0:T(8,128)(2,1)} %weights_ref.3) | copy-start | bytes 6291460
  0.6 6.3 %copy-start.2 = (s32[16,16]{1,0:T(8,128)S(1)}, s32[16,16]{1,0:T(8,128)}, u32[]{:S(2)}) copy-start(s32[16,16]{1,0:T(8,128)} %lists_hbm.1) | copy-start | bytes 3076
  0.7 6.3 %copy-start.4 = (s32[128]{0:T(128)S(1)}, s32[128]{0:T(128)}, u32[]{:S(2)}) copy-start(s32[128]{0:T(128)} %slot_hbm.1) | copy-start | bytes 1540
  0.7 7.9 %copy-start = (bf16[512,1024]{1,0:T(8,128)(2,1)S(1)}, bf16[512,1024]{1,0:T(8,128)(2,1)}, u32[]{:S(2)}) copy-start(bf16[512,1024]{1,0:T(8,128)(2,1)} %param.5) | copy-start | bytes 3145732
  0.7 7.9 %copy-start.3 = (s32[512,8]{0,1:T(8,128)S(1)}, s32[512,8]{0,1:T(8,128)}, u32[]{:S(2)}) copy-start(s32[512,8]{0,1:T(8,128)} %param.9) | copy-start | bytes 49156
  3.7 16.0 %collective-permute-start.2 = (bf16[256,1024]{1,0:T(8,128)(2,1)}, bf16[256,1024]{1,0:T(8,128)(2,1)S(1)}, u32[]{:S(2)}, u32[]{:S(2)}) collective-permute-start(bf16[256,1024]{1,0:T(8,128)(2,1)} %get-tuple-element.37), channel_id=1, source_target_pairs={{0,16},{8,24},{16,0},{24,8},{1,17},{9,25},{17,1},{25,9},{2,18},{10... | collective-permute-start | bytes 1572872 | tf_op jit(solution)/shard_map/ppermute | solution.py:373
  6.7 14.1 %collective-permute-start.1 = (bf16[256,1024]{1,0:T(8,128)(2,1)}, bf16[256,1024]{1,0:T(8,128)(2,1)S(1)}, u32[]{:S(2)}, u32[]{:S(2)}) collective-permute-start(bf16[256,1024]{1,0:T(8,128)(2,1)} %get-tuple-element.36), channel_id=1, source_target_pairs={{0,8},{8,0},{16,24},{24,16},{1,9},{9,1},{17,25},{25,17},{2,10},{10... | collective-permute-start | bytes 1572872 | tf_op jit(solution)/shard_map/ppermute | solution.py:373
  6.7 22.7 %collective-permute-start = (bf16[256,1024]{1,0:T(8,128)(2,1)}, bf16[256,1024]{1,0:T(8,128)(2,1)S(1)}, u32[]{:S(2)}, u32[]{:S(2)}) collective-permute-start(bf16[256,1024]{1,0:T(8,128)(2,1)} %get-tuple-element.34), channel_id=1, source_target_pairs={{0,24},{8,16},{16,8},{24,0},{1,25},{9,17},{17,9},{25,1},{2,26},{10... | collective-permute-start | bytes 1572872 | tf_op jit(solution)/shard_map/ppermute | solution.py:373
  44.8 7.5 %collective-permute-start.3 = (bf16[4,256,128]{2,1,0:T(8,128)(2,1)S(1)}, bf16[4,256,128]{2,1,0:T(8,128)(2,1)S(1)}, u32[]{:S(2)}, u32[]{:S(2)}) collective-permute-start(bf16[4,256,128]{2,1,0:T(8,128)(2,1)S(1)} %get-tuple-element.46), channel_id=1, source_target_pairs={{0,1},{1,0},{2,3},{3,2},{4,5},{5,4},{6,7},{7,6},{8,9},{9,8},{10,11... | collective-permute-start | bytes 786440 | tf_op jit(solution)/shard_map/ppermute | solution.py:478
  52.3 6.6 %collective-permute-start.7 = (bf16[4,256,128]{2,1,0:T(8,128)(2,1)S(1)}, bf16[4,256,128]{2,1,0:T(8,128)(2,1)S(1)}, u32[]{:S(2)}, u32[]{:S(2)}) collective-permute-start(bf16[4,256,128]{2,1,0:T(8,128)(2,1)S(1)} %get-tuple-element.53), channel_id=1, source_target_pairs={{0,1},{1,0},{2,3},{3,2},{4,5},{5,4},{6,7},{7,6},{8,9},{9,8},{10,11... | collective-permute-start | bytes 786440 | tf_op jit(solution)/shard_map/ppermute | solution.py:478
  52.8 7.5 %collective-permute-start.4 = (bf16[256,128]{1,0:T(8,128)(2,1)S(1)}, bf16[256,128]{1,0:T(8,128)(2,1)S(1)}, u32[]{:S(2)}, u32[]{:S(2)}) collective-permute-start(bf16[256,128]{1,0:T(8,128)(2,1)S(1)} %get-tuple-element.48), channel_id=1, source_target_pairs={{0,2},{1,3},{2,0},{3,1},{4,6},{5,7},{6,4},{7,5},{8,10},{9,11},{10,... | collective-permute-start | bytes 196616 | tf_op jit(solution)/shard_map/ppermute | solution.py:491
  53.6 9.8 %collective-permute-start.5 = (bf16[256,128]{1,0:T(8,128)(2,1)S(1)}, bf16[256,128]{1,0:T(8,128)(2,1)S(1)}, u32[]{:S(2)}, u32[]{:S(2)}) collective-permute-start(bf16[256,128]{1,0:T(8,128)(2,1)S(1)} %get-tuple-element.49), channel_id=1, source_target_pairs={{0,4},{1,5},{2,6},{3,7},{4,0},{5,1},{6,2},{7,3},{8,12},{9,13},{10,... | collective-permute-start | bytes 196616 | tf_op jit(solution)/shard_map/ppermute | solution.py:491
  54.6 8.8 %collective-permute-start.6 = (bf16[256,128]{1,0:T(8,128)(2,1)S(1)}, bf16[256,128]{1,0:T(8,128)(2,1)S(1)}, u32[]{:S(2)}, u32[]{:S(2)}) collective-permute-start(bf16[256,128]{1,0:T(8,128)(2,1)S(1)} %get-tuple-element.50), channel_id=1, source_target_pairs={{0,6},{1,7},{2,4},{3,5},{4,2},{5,3},{6,0},{7,1},{8,14},{9,15},{10,... | collective-permute-start | bytes 196616 | tf_op jit(solution)/shard_map/ppermute | solution.py:491
  58.9 6.3 %collective-permute-start.10 = (bf16[256,128]{1,0:T(8,128)(2,1)S(1)}, bf16[256,128]{1,0:T(8,128)(2,1)S(1)}, u32[]{:S(2)}, u32[]{:S(2)}) collective-permute-start(bf16[256,128]{1,0:T(8,128)(2,1)S(1)} %get-tuple-element.57), channel_id=1, source_target_pairs={{0,6},{1,7},{2,4},{3,5},{4,2},{5,3},{6,0},{7,1},{8,14},{9,15},{10,... | collective-permute-start | bytes 196616 | tf_op jit(solution)/shard_map/ppermute | solution.py:491
  59.8 6.2 %collective-permute-start.8 = (bf16[256,128]{1,0:T(8,128)(2,1)S(1)}, bf16[256,128]{1,0:T(8,128)(2,1)S(1)}, u32[]{:S(2)}, u32[]{:S(2)}) collective-permute-start(bf16[256,128]{1,0:T(8,128)(2,1)S(1)} %get-tuple-element.55), channel_id=1, source_target_pairs={{0,2},{1,3},{2,0},{3,1},{4,6},{5,7},{6,4},{7,5},{8,10},{9,11},{10,... | collective-permute-start | bytes 196616 | tf_op jit(solution)/shard_map/ppermute | solution.py:491
  60.3 5.7 %collective-permute-start.9 = (bf16[256,128]{1,0:T(8,128)(2,1)S(1)}, bf16[256,128]{1,0:T(8,128)(2,1)S(1)}, u32[]{:S(2)}, u32[]{:S(2)}) collective-permute-start(bf16[256,128]{1,0:T(8,128)(2,1)S(1)} %get-tuple-element.56), channel_id=1, source_target_pairs={{0,4},{1,5},{2,6},{3,7},{4,0},{5,1},{6,2},{7,3},{8,12},{9,13},{10,... | collective-permute-start | bytes 196616 | tf_op jit(solution)/shard_map/ppermute | solution.py:491
